TPU v7x, 32 devices: a whole 2x2x4 slice. The times are simulated.
32 devices in a mesh: grp: 2 (over x), wide: 16 (over z, y, core).
Axes of the slice: x: 2, y: 2, z: 4, core: 2. Of those that a mesh axis runs over, the one named last changes fastest.
Arguments:
- query_rows: bfloat16 [2048, 2048], P(('grp', 'wide')), parts along dimension 0, may hold values from -10 to 10
- row_key_value: bfloat16 [2048, 512], P(('grp', 'wide')), parts along dimension 0, may hold values from -6 to 6
- key_value_cache: bfloat16 [65536, 512], P(('grp', 'wide')), parts along dimension 0, may hold values from -5 to 5
- resid: bfloat16 [2048, 2048], P(('grp', 'wide')), parts along dimension 0, may hold values from -12 to 12
- norm_gain: float32 [2048], replicated, may hold values from 0.5 to 1.5
- lengths: int32 [16], P('grp'), parts along dimension 0, may hold values from 1024 to 4096, as said below
- positions: int32 [16, 128], P('grp'), parts along dimension 0, may hold values from 0 to 4095, as said below
- expert_ids: int32 [2048, 8], P(('grp', 'wide')), parts along dimension 0, may hold values from 0 to 15, all different within a row; in each aligned block of 64 rows (0 to 63, 64 to 127, ...) at most 48 rows name the same one
- gate_scores: float32 [2048, 8], P(('grp', 'wide')), parts along dimension 0, may hold values from 0.1 to 1
- w_gate: bfloat16 [16, 2048, 768], P('wide'), may hold values from -0.125 to 0.125
- w_up: bfloat16 [16, 2048, 768], P('wide'), may hold values from -0.125 to 0.125
- w_down: bfloat16 [16, 768, 2048], P('wide'), may hold values from -0.21875 to 0.21875
Outputs:
- out_rows: bfloat16 [2048, 2048], P(('grp', 'wide')), parts along dimension 0
There are 2 independent parts, one for each index of `grp`. A program takes and returns all parts, laid end to end along the dimension named above; an argument that names none is the same for every part. Nothing has to cross between parts.
Inputs may be any that keep to these rules, and one draw needn't show every extreme that they name: `lengths`: one document has length exactly 4096 and another exactly 1024. Within a document the positions are distinct and below its length. `expert_ids`: the 64 rows of one device name each expert at most 48 times, and some expert exactly that often.
All inputs are finite; a program needn't handle non-finite values.
Results may differ from a plain program's by a relative error of at most 0.0095.
Values may be sent and summed in bfloat16 or wider, within the bound.
A program may use at most 128 MiB of HBM per device.

v0:
```python
import math

import jax
import jax.numpy as jnp
from jax import lax
from jax.sharding import PartitionSpec as P

QUERY_HEADS = 32
KEY_VALUE_HEADS = 4
HEAD_SIZE = 64


score_masked_rows = -1e30


def swapped(shard, axis, bit):
    return lax.ppermute(shard, axis, [(i, i ^ 1 << bit) for i in range(lax.axis_size(axis))])


def empty_state(masked_row_count):
    query_group_width = QUERY_HEADS // KEY_VALUE_HEADS
    return (
        jnp.zeros((masked_row_count, KEY_VALUE_HEADS, query_group_width, HEAD_SIZE), jnp.float32),
        jnp.full(
            (masked_row_count, KEY_VALUE_HEADS, query_group_width), score_masked_rows, jnp.float32
        ),
        jnp.zeros((masked_row_count, KEY_VALUE_HEADS, query_group_width), jnp.float32),
    )


def split_heads(query_matrix):
    return query_matrix.reshape(
        query_matrix.shape[0], KEY_VALUE_HEADS, QUERY_HEADS // KEY_VALUE_HEADS, HEAD_SIZE
    )


def attend_block(softmax_state, query_head_rows, key_tile_block, usable):
    accumulated, running_max, denominator = softmax_state
    key_value_width = KEY_VALUE_HEADS * HEAD_SIZE
    key_portion = key_tile_block[:, :key_value_width].reshape(
        key_tile_block.shape[0], KEY_VALUE_HEADS, HEAD_SIZE
    )
    value_portion = key_tile_block[:, key_value_width:].reshape(
        key_tile_block.shape[0], KEY_VALUE_HEADS, HEAD_SIZE
    )
    scores = jnp.einsum(
        "mgqd,lgd->mgql", query_head_rows, key_portion, preferred_element_type=jnp.float32
    ) * (1.0 / math.sqrt(HEAD_SIZE))
    if usable is not None:
        scores = jnp.where(usable, scores, score_masked_rows)
    new_max = jnp.maximum(running_max, jnp.max(scores, axis=-1))
    weights = jnp.exp(scores - new_max[..., None])
    if usable is not None:
        weights = jnp.where(usable, weights, 0.0)
    rescale = jnp.exp(running_max - new_max)
    denominator = denominator * rescale + jnp.sum(weights, axis=-1)
    accumulated = accumulated * rescale[..., None] + jnp.einsum(
        "mgql,lgd->mgqd",
        weights.astype(jnp.bfloat16),
        value_portion,
        preferred_element_type=jnp.float32,
    )
    return (accumulated, new_max, denominator)


def attend_cache(softmax_state, query_head_rows, cache_rows, start, length, marked):
    cache_span = cache_rows.shape[0]
    block_size = min(cache_span, 1024)
    block_count = cache_span // block_size
    blocks = cache_rows.reshape(block_count, block_size, cache_rows.shape[1])

    def cache_step(carried, element):
        block_index, key_tile_block = element
        location = start + block_index * block_size + jnp.arange(block_size, dtype=jnp.int32)
        is_marked = jnp.any(location[:, None] == marked[None, :], axis=1)
        usable = (location < length) & ~is_marked
        return (attend_block(carried, query_head_rows, key_tile_block, usable), None)

    softmax_state, unused = lax.scan(
        cache_step, softmax_state, (jnp.arange(block_count, dtype=jnp.int32), blocks)
    )
    return softmax_state


def local_part(query_matrix, row_key_value, key_value_cache, start, length, marked):
    query_head_rows = split_heads(query_matrix)
    softmax_state = attend_block(
        empty_state(query_matrix.shape[0]), query_head_rows, row_key_value, None
    )
    return attend_cache(softmax_state, query_head_rows, key_value_cache, start, length, marked)


def normalize_state(softmax_state, masked_row_count):
    accumulated, running_max, denominator = softmax_state
    return (
        (accumulated / denominator[..., None])
        .reshape(masked_row_count, QUERY_HEADS * HEAD_SIZE)
        .astype(jnp.bfloat16)
    )


def local(
    query_rows,
    row_key_value,
    key_value_cache,
    resid,
    norm_gain,
    lengths,
    positions,
    expert_ids,
    gate_scores,
    w_gate,
    w_up,
    w_down,
):
    masked_row_count = query_rows.shape[0]
    cache_span = key_value_cache.shape[0]
    query_group_width = QUERY_HEADS // KEY_VALUE_HEADS
    device = lax.axis_index("wide")
    doc_index = device // 2
    half_index = device % 2
    length = lax.dynamic_index_in_dim(lengths, doc_index, 0, keepdims=False)
    marked = lax.dynamic_index_in_dim(positions, doc_index, 0, keepdims=False)
    own_sum, own_max, own_total = local_part(
        query_rows, row_key_value, key_value_cache, half_index * cache_span, length, marked
    )
    visitor = swapped(query_rows, "wide", 0)
    hosted_sum, hosted_max, hosted_total = local_part(
        visitor, row_key_value, key_value_cache, half_index * cache_span, length, marked
    )
    far_sum, far_max, far_total = (
        swapped(
            hosted_sum.reshape(masked_row_count, QUERY_HEADS * HEAD_SIZE).astype(jnp.bfloat16),
            "wide",
            0,
        ).astype(jnp.float32),
        swapped(
            hosted_max.reshape(masked_row_count, QUERY_HEADS).astype(jnp.bfloat16), "wide", 0
        ).astype(jnp.float32),
        swapped(
            hosted_total.reshape(masked_row_count, QUERY_HEADS).astype(jnp.bfloat16), "wide", 0
        ).astype(jnp.float32),
    )
    far_sum = far_sum.reshape(masked_row_count, KEY_VALUE_HEADS, query_group_width, HEAD_SIZE)
    far_max = far_max.reshape(masked_row_count, KEY_VALUE_HEADS, query_group_width)
    far_total = far_total.reshape(masked_row_count, KEY_VALUE_HEADS, query_group_width)
    joint_max = jnp.maximum(own_max, far_max)
    own_scale = jnp.exp(own_max - joint_max)
    far_scale = jnp.exp(far_max - joint_max)
    merged_sum = own_sum * own_scale[..., None] + far_sum * far_scale[..., None]
    merged_total = own_total * own_scale + far_total * far_scale
    attention_output = normalize_state((merged_sum, joint_max, merged_total), masked_row_count)
    model_width = resid.shape[1]
    residual = resid.astype(jnp.float32) + attention_output.astype(jnp.float32)
    normed = (
        residual
        * lax.rsqrt(jnp.mean(residual * residual, axis=-1, keepdims=True) + 1e-06)
        * norm_gain
    ).astype(jnp.bfloat16)
    mix = gate_scores / jnp.sum(gate_scores, axis=-1, keepdims=True)
    experts = lax.axis_size("wide")
    chosen_count = expert_ids.shape[1]
    capacity = max(
        2, min(masked_row_count * 3 // 4, masked_row_count * chosen_count * 2 // experts)
    )
    one_hot = (expert_ids[..., None] == jnp.arange(experts, dtype=jnp.int32)).astype(jnp.int32)
    member = jnp.sum(one_hot, axis=1)
    before = jnp.cumsum(member, axis=0) - member
    slot_index = jnp.sum(one_hot * before[:, None, :], axis=-1)
    target = expert_ids * capacity + slot_index
    dispatch = jnp.any(
        target[..., None] == jnp.arange(experts * capacity, dtype=jnp.int32), axis=1
    ).astype(jnp.bfloat16)
    outbound = jnp.einsum("rs,rd->sd", dispatch, normed, preferred_element_type=jnp.float32).astype(
        jnp.bfloat16
    )
    outbound = outbound.reshape(experts, capacity, model_width)
    arrived = lax.all_to_all(outbound, "wide", split_axis=0, concat_axis=0, tiled=True)
    flat_rows = arrived.reshape(-1, model_width)
    gate_act = jnp.dot(flat_rows, w_gate[0], preferred_element_type=jnp.float32)
    up_act = jnp.dot(flat_rows, w_up[0], preferred_element_type=jnp.float32)
    hidden = (jax.nn.silu(gate_act) * up_act).astype(jnp.bfloat16)
    expert_out = jnp.dot(hidden, w_down[0], preferred_element_type=jnp.float32).astype(jnp.bfloat16)
    results = expert_out.reshape(arrived.shape[0], arrived.shape[1], model_width)
    returned = lax.all_to_all(results, "wide", split_axis=0, concat_axis=0, tiled=True).reshape(
        experts * capacity, model_width
    )
    picked = jnp.take(returned, target.reshape(-1), axis=0).reshape(
        masked_row_count, chosen_count, model_width
    )
    routed_sum = jnp.sum(mix[..., None] * picked.astype(jnp.float32), axis=1)
    return (residual + routed_sum).astype(jnp.bfloat16)


def solution(mesh):
    return jax.shard_map(
        local,
        mesh=mesh,
        in_specs=(
            P(("grp", "wide"), None),
            P(("grp", "wide"), None),
            P(("grp", "wide"), None),
            P(("grp", "wide"), None),
            P(),
            P("grp"),
            P("grp", None),
            P(("grp", "wide"), None),
            P(("grp", "wide"), None),
            P("wide", None, None),
            P("wide", None, None),
            P("wide", None, None),
        ),
        out_specs=P(("grp", "wide"), None),
        check_vma=False,
    )
```

profile of v0, /device:TPU:13, one launch (start us, length us, event | category | flops | bytes accessed | tf_op | source)
XLA Modules:
  0.0 275.1 jit_solution(9714733115089388596)
XLA Ops:
  0.7 2.5 reshape.171
  5.2 1.3 dynamic_slice.22
  7.2 4.0 %copy.47 = bf16[2,1024,512]{1,2,0:T(8,128)(2,1)} copy(bf16[2,1024,512]{2,1,0:T(8,128)(2,1)} %bitcast.188) | data formatting | bytes 4194304 | tf_op jit(solution)/shard_map/while | solution.py:79
  11.2 2.0 copy.43
  13.2 1.7 fusion.79
  15.2 1.5 fusion.42
  16.7 2.5 copy.46
  19.2 26.0 %while.28 = (s32[]{:T(128)}, f32[64,4,8,64]{0,3,2,1:T(8,128)}, f32[64,4,8]{0,2,1:T(8,128)S(1)}, f32[64,4,8]{0,2,1:T(8,128)S(1)}, s32[2]{0:T(128)S(1)}, /*index=5...) while((s32[]{:T(128)}, f32[64,4,8,64]{0,3,2,1:T(8,128)}, ...), condition=%wide.region_6.7_spmd, body=%wide.region_2.6_spmd.sunk | while | flops 564666368 | bytes 38157060 | solution.py:79
  19.2 1.3 dynamic-slice_bitcast_fusion.5
  20.5 1.1 fusion.107
  23.9 2.5 bitcast_reduce_fusion.4
  26.4 2.3 fusion.108
  28.8 2.5 fusion.109
  32.2 1.3 dynamic-slice_bitcast_fusion.5
  33.5 1.1 fusion.107
  36.9 2.5 bitcast_reduce_fusion.4
  39.4 2.3 fusion.108
  41.8 2.5 fusion.109
  45.9 2.3 reshape.174
  48.2 1.7 fusion.78
  49.9 2.1 copy.50
  52.2 1.5 fusion.43
  53.7 2.5 copy.53
  56.2 25.9 %while.29 = (s32[]{:T(128)}, f32[64,4,8,64]{0,3,2,1:T(8,128)}, f32[64,4,8]{0,2,1:T(8,128)S(1)}, f32[64,4,8]{0,2,1:T(8,128)S(1)}, s32[2]{0:T(128)S(1)}, /*index=5...) while((s32[]{:T(128)}, f32[64,4,8,64]{0,3,2,1:T(8,128)}, ...), condition=%wide.region_13.14_spmd, body=%wide.region_9.13_spmd.sunk | while | flops 564666368 | bytes 38157060 | solution.py:79
  56.2 1.3 dynamic-slice_bitcast_fusion.6
  57.5 1.0 fusion.114
  60.8 2.5 bitcast_reduce_fusion.5
  63.4 2.3 fusion.115
  65.7 2.5 fusion.116
  69.2 1.3 dynamic-slice_bitcast_fusion.6
  73.7 2.5 bitcast_reduce_fusion.5
  76.3 2.3 fusion.115
  78.6 2.5 fusion.116
  82.1 1.3 convert_element_type.73
  85.4 1.5 fusion.48
  86.9 1.1 bitcast_convert_fusion
  88.0 2.4 copy.82
  90.4 1.2 multiply_reduce_fusion.1
  91.7 2.1 convolution_convert_fusion.1
  93.8 75.9 %all_to_all.10 = bf16[16,48,2048]{2,1,0:T(8,128)(2,1)S(1)} all-to-all(bf16[16,48,2048]{2,1,0:T(8,128)(2,1)S(1)} %bitcast.184), channel_id=1, replica_groups=mesh['grp'=2,'wide'=16] {'wide'}, dimensions={0} | all-to-all | bytes 6291456 | tf_op jit(solution)/shard_map/all_to_all | solution.py:178
  169.6 1.7 copy-done.7
  171.3 4.0 %fusion.35 = f32[768,768]{1,0:T(8,128)} fusion(bf16[768,2048]{1,0:T(8,128)(2,1)S(1)} %bitcast.186, bf16[1,2048,768]{2,1,0:T(8,128)(2,1)S(1)} %copy-done.13), kind=kOutput, calls=%fused_computation.47 | convolution fusion | flops 2415919104 | bytes 8650752 | tf_op jit(solution)/shard_map/dot_general | solution.py:181
  175.4 11.0 %convolution_convert_fusion = bf16[768,2048]{1,0:T(8,128)(2,1)} fusion(bf16[1,768,2048]{2,1,0:T(8,128)(2,1)S(1)} %copy-done, f32[768,768]{1,0:T(8,128)} %fusion.35, bf16[768,2048]{1,0:T(8,128)(2,1)} %bitcast.187, bf16[1,2048,768]{2,1,0:T(8,128)(2,1)} %param.25), kind=kOutput, calls=%fused_computation.44 | convolution fusion | flops 4836950016 | bytes 14942208 | tf_op jit(solution)/shard_map/dot_general | solution.py:183
  186.4 5.3 %all-to-all-start.1 = ((bf16[16,48,2048]{2,1,0:T(8,128)(2,1)}), bf16[16,48,2048]{2,1,0:T(8,128)(2,1)}, u32[]{:S(2)}, u32[]{:S(2)}) async-start(bf16[16,48,2048]{2,1,0:T(8,128)(2,1)} %bitcast.185), calls=%async_computation.1 | async-start | bytes 6291456 | tf_op jit(solution)/shard_map/all_to_all | solution.py:185
  192.0 69.6 %all-to-all-done.1 = bf16[16,48,2048]{2,1,0:T(8,128)(2,1)} async-done(((bf16[16,48,2048]{2,1,0:T(8,128)(2,1)}), bf16[16,48,2048]{2,1,0:T(8,128)(2,1)}, u32[]{:S(2)}, u32[]{:S(2)}) %all-to-all-start.1) | async-done | bytes 3145760 | tf_op jit(solution)/shard_map/all_to_all | solution.py:185
  261.7 7.6 %gather_fusion = bf16[512,2048]{1,0:T(8,128)(2,1)} fusion(bf16[768,2048]{1,0:T(8,128)(2,1)} %bitcast.45, s32[1024]{0:T(1024)S(1)} %pad_clamp_fusion), kind=kCustom, calls=%fused_computation | custom fusion | bytes 4196352 | tf_op jit(solution)/shard_map/jit(_take)/gather | solution.py:188
  269.3 4.0 %multiply_reduce_fusion = f32[64,2048]{1,0:T(8,128)S(1)} fusion(bf16[512,2048]{1,0:T(8,128)(2,1)} %gather_fusion, f32[64,8]{1,0:T(8,128)S(1)} %copy.57, pred[64,8]{1,0:T(8,128)(4,1)S(1)} %copy.61), kind=kLoop, calls=%fused_computation.43 | loop fusion | flops 4063232 | bytes 2624000 | tf_op jit(solution)/shard_map/reduce_sum | solution.py:191
  273.2 1.8 add_convert_fusion
  (108 shorter events, 18.4 us)
Async XLA Ops:
  0.0 175.4 %copy-start = (bf16[1,768,2048]{2,1,0:T(8,128)(2,1)S(1)}, bf16[1,768,2048]{2,1,0:T(8,128)(2,1)}, u32[]{:S(2)}) copy-start(bf16[1,768,2048]{2,1,0:T(8,128)(2,1)} %param.27) | copy-start | bytes 9437188
  0.0 45.9 %collective-permute-start = (bf16[64,2048]{1,0:T(8,128)(2,1)}, bf16[64,2048]{1,0:T(8,128)(2,1)}, u32[]{:S(2)}, u32[]{:S(2)}) collective-permute-start(bf16[64,2048]{1,0:T(8,128)(2,1)} %param.16), channel_id=1, source_target_pairs={{0,1},{1,0},{2,3},{3,2},{4,5},{5,4},{6,7},{7,6},{8,9},{9,8},{10,11... | collective-permute-start | bytes 786440 | tf_op jit(solution)/shard_map/ppermute | solution.py:17
  19.2 26.0 %copy-start.9 = (s32[64,8]{0,1:T(8,128)S(1)}, s32[64,8]{0,1:T(8,128)}, u32[]{:S(2)}) copy-start(s32[64,8]{0,1:T(8,128)} %param.23) | copy-start | bytes 6148
  26.4 2.3 copy-start.1
  26.4 2.3 copy-start.3
  31.2 1.0 copy-start.4
  39.4 2.3 copy-start.1
  39.4 2.3 copy-start.3
  44.2 1.0 copy-start.4
  63.3 2.3 copy-start.2
  63.4 2.3 copy-start.5
  68.2 1.0 copy-start.6
  76.3 2.3 copy-start.2
  76.3 2.3 copy-start.5
  81.1 1.0 copy-start.6
  83.4 7.0 %copy-start.8 = (bf16[64,2048]{1,0:T(8,128)(2,1)S(1)}, bf16[64,2048]{1,0:T(8,128)(2,1)}, u32[]{:S(2)}) copy-start(bf16[64,2048]{1,0:T(8,128)(2,1)} %param.19) | copy-start | bytes 786436
  83.4 2.0 collective-permute-start.2
  83.5 1.9 collective-permute-start.3
  84.0 7.7 %copy-start.11 = (f32[2048]{0:T(1024)S(1)}, f32[2048]{0:T(1024)}, u32[]{:S(2)}) copy-start(f32[2048]{0:T(1024)} %param.20) | copy-start | bytes 24580
  84.0 1.4 collective-permute-start.1
  93.7 77.6 %copy-start.13 = (bf16[1,2048,768]{2,1,0:T(8,128)(2,1)S(1)}, bf16[1,2048,768]{2,1,0:T(8,128)(2,1)}, u32[]{:S(2)}) copy-start(bf16[1,2048,768]{2,1,0:T(8,128)(2,1)} %param.26) | copy-start | bytes 9437188
  169.6 1.7 copy-start.7
  186.4 5.4 %copy-start.10 = (f32[64,8]{0,1:T(8,128)S(1)}, f32[64,8]{0,1:T(8,128)}, u32[]{:S(2)}) copy-start(f32[64,8]{0,1:T(8,128)} %param.24) | copy-start | bytes 6148
  186.4 5.5 %copy-start.12 = (pred[64,8]{0,1:T(8,128)(4,1)S(1)}, pred[64,8]{0,1:T(8,128)(4,1)}, u32[]{:S(2)}) copy-start(pred[64,8]{0,1:T(8,128)(4,1)} %get-tuple-element.223) | copy-start | bytes 1540
  186.4 75.3 %all-to-all-start.1 = ((bf16[16,48,2048]{2,1,0:T(8,128)(2,1)}), bf16[16,48,2048]{2,1,0:T(8,128)(2,1)}, u32[]{:S(2)}, u32[]{:S(2)}) async-start(bf16[16,48,2048]{2,1,0:T(8,128)(2,1)} %bitcast.185), calls=%async_computation.1 | async-start | bytes 6291456 | tf_op jit(solution)/shard_map/all_to_all | solution.py:185
where the time goes:
time: 276 us; the launch traced here: 275 us
  blocking collectives  75.9 us (28%)
  waiting for transfers between devices  70.4 us (26%)
  local copies, waits for them, and re-layouts  48.8 us (18%)
  matrix products  43.5 us (16%)
  other arithmetic  26.8 us (10%)
  starting transfers between devices  6.65 us (2%)
  loops' own time  2.81 us (1%)
    all_to_all x1, blocking collectives, local(): lax.all_to_all(outbound, 'wide', split_axis=0, concat_axis=0, tiled=True)  75.9 us
    all_to_all x1, waiting for transfers between devices, local(): lax.all_to_all(results, 'wide', split_axis=0, concat_axis=0, tiled=True)  69.6 us
    dot_general x6, matrix products, attend_block(): jnp.einsum('mgqd,lgd->mgql', query_head_rows, key_portion, preferred_elem...  13.5 us
    dot_general x6, matrix products, attend_block(): jnp.einsum('mgql,lgd->mgqd', weights.astype(jnp.bfloat16), value_portion,...  12.8 us
    dot_general x1, matrix products, local(): jnp.dot(hidden, w_down[0], preferred_element_type=jnp.float32)  11 us
    reduce_sum x6, other arithmetic, attend_block(): denominator = denominator * rescale + jnp.sum(weights, axis=-1)  9.56 us
    while x3, local copies, waits for them, and re-layouts, attend_cache(): lax.scan(cache_step, softmax_state, (jnp.arange(block_count, dtype=jnp.in...  9.05 us
    reshape x4, local copies, waits for them, and re-layouts, split_heads(): query_matrix.reshape(query_matrix.shape[0], KEY_VALUE_HEADS, QUERY_HEADS...  8.9 us
  transfers between devices with their start and end apart: 5, of which 2 were waited for; matrix products, arithmetic and copies ran while one was open for 15% of the time, Pallas kernels for 0%

commit v1 on v0

v1 whole, which is shorter than its diff:
```python
import functools
import math

import jax
import jax.numpy as jnp
from jax import lax
from jax.experimental import pallas as pl
from jax.experimental.pallas import tpu as pltpu
from jax.sharding import PartitionSpec as P

KEY_VALUE_HEADS = 4
HEAD_SIZE = 64
LANES = 128
NEVER = -1e30


def swapped(shard, axis, bit):
    return lax.ppermute(shard, axis, [(i, i ^ 1 << bit) for i in range(lax.axis_size(axis))])


def lane_index(shape):
    return lax.broadcasted_iota(jnp.int32, shape, 1)


def half_with_one(slab, odd):
    values = slab.astype(jnp.float32)
    if odd:
        values = pltpu.roll(values, HEAD_SIZE, 1)
    lane = lane_index(values.shape)
    return jnp.where(
        lane < HEAD_SIZE, values, jnp.where(lane == HEAD_SIZE, 1.0, 0.0)
    ).astype(jnp.bfloat16)


def attention_kernel(
    start_ref, length_ref, q_ref, cache_ref, rows_ref, marked_ref, out_ref, lse_ref,
    q_scr, k_scr, v_scr, s_scr,
):
    rows = q_ref.shape[0]
    span = cache_ref.shape[0]
    own = rows_ref.shape[0]
    keys = k_scr.shape[2]
    query_heads = q_ref.shape[1] // HEAD_SIZE
    width = KEY_VALUE_HEADS * HEAD_SIZE
    group = query_heads // KEY_VALUE_HEADS

    location = lane_index((1, keys))
    place = start_ref[0] + location
    hit = jnp.max(
        jnp.where(marked_ref[...] == place, 1.0, 0.0), axis=0, keepdims=True
    )
    in_cache = (place < length_ref[0]) & (hit == 0.0) & (location < span)
    usable = in_cache | ((location >= span) & (location < span + own))
    bias = jnp.where(usable, 0.0, NEVER)
    row = lax.broadcasted_iota(jnp.int32, (HEAD_SIZE, keys), 0)
    bias_rows = jnp.where(row == 0, bias, 0.0).astype(jnp.bfloat16)
    pad = keys - span - own
    for slab in range(KEY_VALUE_HEADS // 2):
        columns = slice(slab * LANES, (slab + 1) * LANES)
        value_columns = slice(width + slab * LANES, width + (slab + 1) * LANES)
        tail = [rows_ref[:, columns]]
        value_tail = [rows_ref[:, value_columns]]
        if pad:
            tail.append(jnp.zeros((pad, LANES), jnp.bfloat16))
            value_tail.append(jnp.zeros((pad, LANES), jnp.bfloat16))
        slab_keys = jnp.concatenate([cache_ref[:, columns]] + tail, axis=0).T
        slab_values = jnp.concatenate([cache_ref[:, value_columns]] + value_tail, axis=0)
        for odd in range(2):
            head = 2 * slab + odd
            k_scr[head, :HEAD_SIZE, :] = slab_keys[odd * HEAD_SIZE : (odd + 1) * HEAD_SIZE, :]
            k_scr[head, HEAD_SIZE:, :] = bias_rows
            v_scr[head] = half_with_one(slab_values, odd)
    for pair in range(query_heads // 2):
        slab = q_ref[:, pair * LANES : (pair + 1) * LANES].astype(jnp.float32) * (
            1.0 / math.sqrt(HEAD_SIZE)
        )
        for odd in range(2):
            q_scr[pair, odd * rows : (odd + 1) * rows, :] = half_with_one(slab, odd)

    pairs = query_heads // 2

    def scores(pair, slot):
        head = lax.div(pair, group // 2)
        s_scr[slot] = jnp.dot(q_scr[pair], k_scr[head], preferred_element_type=jnp.float32)

    def finish(pair, slot):
        head = lax.div(pair, group // 2)
        s = s_scr[slot]
        largest = jnp.max(s, axis=1, keepdims=True)
        p = jnp.exp(s - largest).astype(jnp.bfloat16)
        summed = jnp.dot(p, v_scr[head], preferred_element_type=jnp.float32)
        total = summed[:, HEAD_SIZE : HEAD_SIZE + 1]
        mean = summed / total
        lse = jnp.broadcast_to(largest + jnp.log(total), mean.shape)
        low = lane_index((rows, LANES)) < HEAD_SIZE
        out_ref[pair] = jnp.where(
            low, mean[:rows], pltpu.roll(mean[rows:], HEAD_SIZE, 1)
        ).astype(jnp.bfloat16)
        lse_ref[pair] = jnp.where(low, lse[:rows], lse[rows:])

    scores(0, 0)

    def step(j, unused):
        scores(2 * j + 1, 1)
        finish(2 * j, 0)
        scores(jnp.minimum(2 * j + 2, pairs - 1), 0)
        finish(2 * j + 1, 1)
        return unused

    lax.fori_loop(0, pairs // 2, step, 0)


def attention(queries, cache, row_key_value, start, length, marked):
    rows, width = queries.shape
    pairs = width // LANES
    keys = -(-(cache.shape[0] + row_key_value.shape[0]) // LANES) * LANES
    vmem = pl.BlockSpec(memory_space=pltpu.VMEM)
    smem = pl.BlockSpec(memory_space=pltpu.SMEM)
    return pl.pallas_call(
        attention_kernel,
        out_shape=(
            jax.ShapeDtypeStruct((pairs, rows, LANES), jnp.bfloat16),
            jax.ShapeDtypeStruct((pairs, rows, LANES), jnp.float32),
        ),
        in_specs=[smem, smem, vmem, vmem, vmem, vmem],
        out_specs=(vmem, vmem),
        scratch_shapes=[
            pltpu.VMEM((pairs, 2 * rows, LANES), jnp.bfloat16),
            pltpu.VMEM((KEY_VALUE_HEADS, LANES, keys), jnp.bfloat16),
            pltpu.VMEM((KEY_VALUE_HEADS, keys, LANES), jnp.bfloat16),
            pltpu.VMEM((2, 2 * rows, keys), jnp.float32),
        ],
        compiler_params=pltpu.CompilerParams(vmem_limit_bytes=40 * 1024 * 1024),
        cost_estimate=pl.CostEstimate(
            flops=4 * rows * width * keys,
            bytes_accessed=2 * cache.size + 8 * rows * width,
            transcendentals=rows * keys * width // HEAD_SIZE,
        ),
        name="attention",
    )(start, length, queries, cache, row_key_value, marked)


def local(
    query_rows,
    row_key_value,
    key_value_cache,
    resid,
    norm_gain,
    lengths,
    positions,
    expert_ids,
    gate_scores,
    w_gate,
    w_up,
    w_down,
):
    rows = query_rows.shape[0]
    width = query_rows.shape[1]
    span = key_value_cache.shape[0]
    device = lax.axis_index("wide")
    experts = lax.axis_size("wide")
    doc_index = device // 2
    half_index = device % 2

    mix = gate_scores / jnp.sum(gate_scores, axis=-1, keepdims=True)
    chosen = expert_ids[..., None] == jnp.arange(experts, dtype=jnp.int32)
    share = jnp.sum(jnp.where(chosen, mix[..., None], 0.0), axis=1)
    all_share = lax.all_gather(share, "wide", axis=0, tiled=True)

    length = lax.dynamic_slice_in_dim(lengths, doc_index, 1, 0)
    marked = lax.dynamic_index_in_dim(positions, doc_index, 0, keepdims=False)[:, None]
    visitor = swapped(query_rows, "wide", 0)
    start = jnp.reshape(half_index * span, (1,)).astype(jnp.int32)
    means, lse = attention(
        jnp.concatenate([query_rows, visitor], axis=0),
        key_value_cache, row_key_value, start, length, marked,
    )
    far_mean = swapped(means[:, rows:], "wide", 0).astype(jnp.float32)
    far_lse = swapped(lse[:, rows:], "wide", 0)
    own_mean = means[:, :rows].astype(jnp.float32)
    own_lse = lse[:, :rows]
    far_part = 1.0 / (1.0 + jnp.exp(own_lse - far_lse))
    merged = own_mean + (far_mean - own_mean) * far_part
    attended = jnp.swapaxes(merged, 0, 1).reshape(rows, width).astype(jnp.bfloat16)

    residual = resid.astype(jnp.float32) + attended.astype(jnp.float32)
    normed = (
        residual
        * lax.rsqrt(jnp.mean(residual * residual, axis=-1, keepdims=True) + 1e-06)
        * norm_gain
    ).astype(jnp.bfloat16)

    everyone = lax.all_gather(normed, "wide", axis=0, tiled=True)
    weight = lax.dynamic_slice_in_dim(all_share, device, 1, 1)
    gate_act = jnp.dot(everyone, w_gate[0], preferred_element_type=jnp.float32)
    up_act = jnp.dot(everyone, w_up[0], preferred_element_type=jnp.float32)
    hidden = (jax.nn.silu(gate_act) * up_act).astype(jnp.bfloat16)
    expert_out = jnp.dot(hidden, w_down[0], preferred_element_type=jnp.float32)
    weighted = (expert_out * weight).astype(jnp.bfloat16)
    routed = lax.psum_scatter(weighted, "wide", scatter_dimension=0, tiled=True)
    return (residual + routed.astype(jnp.float32)).astype(jnp.bfloat16)


def solution(mesh):
    return jax.shard_map(
        local,
        mesh=mesh,
        in_specs=(
            P(("grp", "wide"), None),
            P(("grp", "wide"), None),
            P(("grp", "wide"), None),
            P(("grp", "wide"), None),
            P(),
            P("grp"),
            P("grp", None),
            P(("grp", "wide"), None),
            P(("grp", "wide"), None),
            P("wide", None, None),
            P("wide", None, None),
            P("wide", None, None),
        ),
        out_specs=P(("grp", "wide"), None),
        check_vma=False,
    )
```

time: 276 us -> 187 us (0.68)
  the two profiles are of different devices: /device:TPU:13 before, /device:TPU:0 now
where the time goes in v1:
time: 187 us
  waiting for transfers between devices  101 us (54%)
  blocking collectives  23.5 us (13%)
  matrix products  20.6 us (11%)
  Pallas kernels  15.2 us (8%)
  between operations  13.6 us (7%)
  local copies, waits for them, and re-layouts  6.88 us (4%)
  other arithmetic  4.73 us (3%)
    reduce_scatter x1, waiting for transfers between devices, local(): routed = lax.psum_scatter(weighted, 'wide', scatter_dimension=0, tiled=True)  71.3 us
    all_gather x1, waiting for transfers between devices, local(): everyone = lax.all_gather(normed, 'wide', axis=0, tiled=True)  28.3 us
    all_gather x1, blocking collectives, local(): all_share = lax.all_gather(share, 'wide', axis=0, tiled=True)  23.5 us
    pallas_call x1, Pallas kernels, attention(): pl.pallas_call(attention_kernel, out_shape=(jax.ShapeDtypeStruct((pairs,...  15.2 us
    dot_general x1, matrix products, local(): expert_out = jnp.dot(hidden, w_down[0], preferred_element_type=jnp.float32)  12.3 us
    dot_general x1, matrix products, local(): up_act = jnp.dot(everyone, w_up[0], preferred_element_type=jnp.float32)  8.3 us
  transfers between devices with their start and end apart: 5, of which 3 were waited for; matrix products, arithmetic and copies ran while one was open for 2% of the time, Pallas kernels for 0%

profile of v1, /device:TPU:0, one launch (start us, length us, event | category | flops | bytes accessed | tf_op | source)
XLA Modules:
  0.0 187.0 jit_solution(17218351042880298371)
XLA Ops:
  6.5 0.0 copy-start
  6.5 0.0 all-gather.3.cloned.1.call-start
  6.5 0.5 collective-permute-start
  7.0 1.5 dynamic_slice.10.length_ref
  8.5 0.7 dynamic-slice_bitcast_fusion
  9.2 0.1 copy.29.marked_ref
  9.3 0.0 collective-permute-done
  9.3 1.0 pad_maximum_fusion.q_ref
  10.3 0.0 copy-start.3
  10.3 1.6 copy-done.3
  11.9 0.0 copy-start.4
  11.9 0.8 copy-done.4
  12.7 0.0 copy-start.6
  12.7 15.2 %attention.1 = (bf16[16,128,128]{2,1,0:T(8,128)(2,1)S(1)}, f32[16,128,128]{2,1,0:T(8,128)S(1)}) custom-call(s32[1]{0:T(128)} %bitcast.start_ref, s32[1]{0:T(128)} %dynamic_slice.10.length_ref, bf16[128,2048]{1,0:T(8,128)(2,1)S(1)} %pad_maximum_fusion.q_ref, bf16[2048,512]{1,0:T(8,128)(2,1)S(1)} %copy-done.3, bf16[64,512]{1,0:T(8,128)(2,1)S(1)} %copy-done.4, ...), custom_call_target="tpu_custom_call" | custom-call | flops 2281701376 | bytes 4194304 | tf_op jit(solution)/shard_map/attention/pallas_call | solution.py:119
  28.0 0.0 copy-start.1
  28.0 0.0 copy-start.2
  28.0 0.0 copy-start.9
  28.0 0.0 copy-start.8
  28.1 0.0 copy-start.10
  28.1 0.1 collective-permute-start.2
  28.2 0.6 collective-permute-start.1
  28.8 1.7 collective-permute-done.1
  30.5 0.0 copy-start.7
  30.5 0.0 collective-permute-done.2
  30.5 0.0 copy-done.6
  30.5 0.0 copy-start.5
  30.5 0.3 multiply_reduce_fusion
  30.8 0.0 copy-done.1
  30.8 0.0 copy-done.2
  30.9 0.3 copy-done.7
  31.2 0.2 copy-done.5
  31.4 0.0 copy-done.9
  31.4 1.0 multiply_convert_fusion.2
  32.3 0.0 all-gather.3.cloned.1.call-update
  32.4 0.0 reduce-scatter.2.cloned.1.call-start
  32.4 0.0 copy-done.8
  32.5 0.0 copy-done.10
  32.5 23.5 %all-gather = f32[16,64,16]{1,2,0:T(8,128)S(1)} all-gather(f32[1,64,16]{1,2,0:T(8,128)S(1)} %bitcast.36), channel_id=1, replica_groups=mesh['grp'=2,'wide'=16] {'wide'}, dimensions={0}, use_global_device_ids=true | all-gather | bytes 69632 | tf_op jit(solution)/shard_map/all_gather | solution.py:168
  56.0 0.7 reshape.23
  56.7 0.8 constant_dynamic-slice_fusion
  57.5 28.3 %all-gather.3.cloned.1.call-done = bf16[1024,2048]{1,0:T(8,128)(2,1)} async-done(((bf16[64,2048]{1,0:T(8,128)(2,1)}), bf16[1024,2048]{1,0:T(8,128)(2,1)}) %all-gather.3.cloned.1.call-update) | async-done | bytes 4194320 | tf_op jit(solution)/shard_map/all_gather | solution.py:193
  85.8 8.3 %fusion.1 = f32[1024,768]{1,0:T(8,128)} fusion(bf16[1024,2048]{1,0:T(8,128)(2,1)} %all-gather.3.cloned.1.call-done, bf16[1,2048,768]{2,1,0:T(8,128)(2,1)} %param.22), kind=kOutput, calls=%fused_computation.2 | convolution fusion | flops 3221225472 | bytes 10485760 | tf_op jit(solution)/shard_map/dot_general | solution.py:196
  94.1 0.0 copy-done
  94.1 12.3 %multiply_convert_fusion = bf16[1024,2048]{1,0:T(8,128)(2,1)} fusion(f32[1024]{0:T(1024)S(1)} %bitcast.37, bf16[1,768,2048]{2,1,0:T(8,128)(2,1)S(1)} %copy-done, f32[1024,768]{1,0:T(8,128)} %fusion.1, bf16[1024,2048]{1,0:T(8,128)(2,1)} %all-gather.3.cloned.1.call-done, bf16[1,2048,768]{2,1,0:T(8,128)(2,1)} %param.21), kind=kOutput, calls=%fused_computation | convolution fusion | flops 6451363840 | bytes 17829888 | tf_op jit(solution)/shard_map/dot_general | solution.py:198
  106.4 0.0 reduce-scatter.2.cloned.1.call-update
  106.5 71.3 %reduce-scatter.2.cloned.1.call-done = bf16[64,2048]{1,0:T(8,128)(2,1)} async-done(((bf16[1024,2048]{1,0:T(8,128)(2,1)}), bf16[64,2048]{1,0:T(8,128)(2,1)}) %reduce-scatter.2.cloned.1.call-update) | async-done | bytes 262160 | tf_op jit(solution)/shard_map/reduce_scatter | solution.py:200
  177.8 2.4 %add_convert_fusion = bf16[64,2048]{1,0:T(8,128)(2,1)} fusion(bf16[64,2048]{1,0:T(8,128)(2,1)} %reduce-scatter.2.cloned.1.call-done, bf16[64,2048]{1,0:T(8,128)(2,1)S(1)} %copy-done.6, f32[16,64,128]{2,1,0:T(8,128)} %copy-done.5, f32[16,128,128]{2,1,0:T(8,128)} %copy-done.1, bf16[16,64,128]{2,1,0:T(8,128)(2,1)} %copy-done.7, bf16[16,128,128]{2,1,0:T(8,128)(2,1)} %copy-done.2), kind=kLoop, calls=%fused_computation.14 | loop fusion | flops 1966080 | bytes 2359296 | tf_op jit(solution)/shard_map/convert_element_type | solution.py:201
  (7 shorter events, 0.2 us)
Async XLA Ops:
  6.5 87.6 %copy-start = (bf16[1,768,2048]{2,1,0:T(8,128)(2,1)S(1)}, bf16[1,768,2048]{2,1,0:T(8,128)(2,1)}, u32[]{:S(2)}) copy-start(bf16[1,768,2048]{2,1,0:T(8,128)(2,1)} %param.23) | copy-start | bytes 9437188
  6.5 79.2 %all-gather.3.cloned.1.call-start = ((), (), s32[]{:S(2)}) async-start(), calls=%async_computation.1 | async-start | bytes 4456448 | tf_op jit(solution)/shard_map/all_gather | solution.py:193
  6.5 2.8 %collective-permute-start = (bf16[64,2048]{1,0:T(8,128)(2,1)}, bf16[64,2048]{1,0:T(8,128)(2,1)S(1)}, u32[]{:S(2)}, u32[]{:S(2)}) collective-permute-start(bf16[64,2048]{1,0:T(8,128)(2,1)} %param.12), channel_id=1, source_target_pairs={{0,1},{1,0},{2,3},{3,2},{4,5},{5,4},{6,7},{7,6},{8,9},{9,8},{10,11... | collective-permute-start | bytes 786440 | tf_op jit(solution)/shard_map/ppermute | solution.py:18
  10.3 1.6 copy-start.3
  11.9 0.8 copy-start.4
  12.7 17.7 %copy-start.6 = (bf16[64,2048]{1,0:T(8,128)(2,1)S(1)}, bf16[64,2048]{1,0:T(8,128)(2,1)}, u32[]{:S(2)}) copy-start(bf16[64,2048]{1,0:T(8,128)(2,1)} %param.15) | copy-start | bytes 786436
  28.0 2.8 %copy-start.1 = (f32[16,128,128]{2,1,0:T(8,128)}, f32[16,128,128]{2,1,0:T(8,128)S(1)}, u32[]{:S(2)}) copy-start(f32[16,128,128]{2,1,0:T(8,128)S(1)} %get-tuple-element.8) | copy-start | bytes 3145732
  28.0 2.8 %copy-start.2 = (bf16[16,128,128]{2,1,0:T(8,128)(2,1)}, bf16[16,128,128]{2,1,0:T(8,128)(2,1)S(1)}, u32[]{:S(2)}) copy-start(bf16[16,128,128]{2,1,0:T(8,128)(2,1)S(1)} %get-tuple-element.7) | copy-start | bytes 1572868
  28.0 3.4 %copy-start.9 = (f32[2048]{0:T(1024)S(1)}, f32[2048]{0:T(1024)}, u32[]{:S(2)}) copy-start(f32[2048]{0:T(1024)} %param.16) | copy-start | bytes 24580
  28.0 4.4 %copy-start.8 = (f32[64,8]{0,1:T(8,128)S(1)}, f32[64,8]{0,1:T(8,128)}, u32[]{:S(2)}) copy-start(f32[64,8]{0,1:T(8,128)} %param.20) | copy-start | bytes 6148
  28.1 4.4 %copy-start.10 = (s32[64,8]{0,1:T(8,128)S(1)}, s32[64,8]{0,1:T(8,128)}, u32[]{:S(2)}) copy-start(s32[64,8]{0,1:T(8,128)} %param.19) | copy-start | bytes 6148
  28.1 2.4 %collective-permute-start.2 = (f32[16,64,128]{2,1,0:T(8,128)S(1)}, f32[16,64,128]{2,1,0:T(8,128)S(1)}, u32[]{:S(2)}, u32[]{:S(2)}) collective-permute-start(f32[16,64,128]{2,1,0:T(8,128)S(1)} %slice.15), channel_id=1, source_target_pairs={{0,1},{1,0},{2,3},{3,2},{4,5},{5,4},{6,7},{7,6},{8,9},{9,8},{10,11... | collective-permute-start | bytes 1572872 | tf_op jit(solution)/shard_map/ppermute | solution.py:18
  28.2 2.2 %collective-permute-start.1 = (bf16[16,64,128]{2,1,0:T(8,128)(2,1)S(1)}, bf16[16,64,128]{2,1,0:T(8,128)(2,1)S(1)}, u32[]{:S(2)}, u32[]{:S(2)}) collective-permute-start(bf16[16,64,128]{2,1,0:T(8,128)(2,1)S(1)} %slice.13), channel_id=1, source_target_pairs={{0,1},{1,0},{2,3},{3,2},{4,5},{5,4},{6,7},{7,6},{8,9},{9,8},{10,11... | collective-permute-start | bytes 786440 | tf_op jit(solution)/shard_map/ppermute | solution.py:18
  30.5 0.7 copy-start.7
  30.5 0.9 copy-start.5
  32.4 145.4 %reduce-scatter.2.cloned.1.call-start = ((), (), s32[]{:S(2)}) async-start(), calls=%async_computation.2 | async-start | bytes 4456448 | tf_op jit(solution)/shard_map/reduce_scatter | solution.py:200
Sparse Core Ops, SparseCore 0:
  32.5 53.2 all-gather.2
  106.6 71.1 reduce-scatter.1

commit v2 on v1

--- a/solution.py
+++ b/solution.py
@@ -140,6 +140,258 @@
     )(start, length, queries, cache, row_key_value, marked)
 
 
+def chip_at(place, chips):
+    return jnp.where(place < chips // 2, 2 * place, 2 * (chips - 1 - place) + 1)
+
+
+def place_of(chip, chips):
+    return jnp.where(chip % 2 == 0, chip // 2, chips - 1 - chip // 2)
+
+
+def experts_kernel(
+    devices, first_ref, gate_hbm, up_hbm, down_hbm, out_ref,
+    x, o, sibling_sums, ring_sums, hidden, w_gate, w_up, w_down,
+    weight_sem, gather_send, gather_recv, share_send, share_recv,
+    pair_send, pair_recv, ring_send, ring_recv,
+):
+    rows, half = first_ref.shape[0], first_ref.shape[0] // 2
+    model = out_ref.shape[1]
+    ff = w_down.shape[0]
+    chips = devices // 2
+    hops = chips // 2
+    me = lax.axis_index("wide")
+    core = me % 2
+    place = place_of(me // 2, chips)
+    sibling = me + 1 - 2 * core
+    right = 2 * chip_at((place + 1) % chips, chips) + core
+    left = 2 * chip_at((place + chips - 1) % chips, chips) + core
+
+    def remote(source, target, send, recv, device):
+        return pltpu.make_async_remote_copy(
+            src_ref=source, dst_ref=target, send_sem=send, recv_sem=recv,
+            device_id={"wide": device}, device_id_type=pl.DeviceIdType.MESH,
+        )
+
+    loads = [
+        pltpu.make_async_copy(source.at[0], target, weight_sem.at[i])
+        for i, (source, target) in enumerate(
+            ((gate_hbm, w_gate), (up_hbm, w_up), (down_hbm, w_down))
+        )
+    ]
+    for load in loads:
+        load.start()
+    x[0, :rows] = first_ref[...]
+    ring_sums[hops - 1, half : rows + half] = jnp.zeros((rows, model), jnp.bfloat16)
+
+    barrier = pltpu.get_barrier_semaphore()
+    for neighbour in (left, right, sibling):
+        pl.semaphore_signal(
+            barrier, inc=1, device_id={"wide": neighbour}, device_id_type=pl.DeviceIdType.MESH
+        )
+    pl.semaphore_wait(barrier, 3)
+
+    def gather(hop):
+        if isinstance(hop, int) and hop == hops:
+            top, bottom = pl.ds(0, half), pl.ds(half, half)
+            from_left, from_right = top, bottom if hop == 1 else pl.ds(rows + half, half)
+        else:
+            top = bottom = None
+            from_left, from_right = pl.ds(0, rows), pl.ds(rows, rows)
+            if isinstance(hop, int) and hop == 1:
+                from_right = pl.ds(0, rows)
+        to_left = pl.ds(0, rows) if top is None else top
+        to_right = pl.ds(rows, rows) if bottom is None else bottom
+        return (
+            remote(x.at[hop - 1, from_left], x.at[hop, to_left],
+                   gather_send.at[0, hop], gather_recv.at[0, hop], right),
+            remote(x.at[hop - 1, from_right], x.at[hop, to_right],
+                   gather_send.at[1, hop], gather_recv.at[1, hop], left),
+        )
+
+    def share(hop, count):
+        return remote(x.at[hop, pl.ds(0, count)], x.at[hop, pl.ds(count, count)],
+                      share_send.at[hop], share_recv.at[hop], sibling)
+
+    def pair(hop, count):
+        return remote(o.at[hop, pl.ds(count, count)], sibling_sums.at[hop, pl.ds(0, count)],
+                      pair_send.at[hop], pair_recv.at[hop], sibling)
+
+    def ring(hop):
+        if isinstance(hop, int) and hop == hops:
+            go_left = land_left = pl.ds(0, half)
+            go_right, land_right = pl.ds(half, half), pl.ds(rows + half, half)
+        else:
+            go_left = land_left = pl.ds(0, rows)
+            go_right = land_right = pl.ds(rows, rows)
+        return (
+            remote(o.at[hop, go_left], ring_sums.at[hop - 1, land_left],
+                   ring_send.at[0, hop], ring_recv.at[0, hop], left),
+            remote(o.at[hop, go_right], ring_sums.at[hop - 1, land_right],
+                   ring_send.at[1, hop], ring_recv.at[1, hop], right),
+        )
+
+    def chunk_of(size):
+        return next(c for c in (256, 128, size) if size % c == 0)
+
+    def run_experts(hop, count):
+        tail = x[hop, :count, model:].astype(jnp.float32)
+        lane = lane_index(tail.shape)
+        weight = jnp.sum(
+            jnp.where((lane == me) | (lane == devices + me), tail, 0.0), axis=1, keepdims=True
+        )
+        step = chunk_of(ff)
+
+        def hide(i, unused):
+            columns = pl.ds(pl.multiple_of(i * step, step), step)
+            rows_in = x[hop, :count, :model]
+            g = jnp.dot(rows_in, w_gate[:, columns], preferred_element_type=jnp.float32)
+            u = jnp.dot(rows_in, w_up[:, columns], preferred_element_type=jnp.float32)
+            hidden[:count, columns] = (g / (1.0 + jnp.exp(-g)) * u).astype(jnp.bfloat16)
+            return unused
+
+        lax.fori_loop(0, ff // step, hide, 0)
+        wide = chunk_of(model)
+
+        def expand(i, unused):
+            columns = pl.ds(pl.multiple_of(i * wide, wide), wide)
+            y = jnp.dot(hidden[:count], w_down[:, columns], preferred_element_type=jnp.float32)
+            o[hop, :count, columns] = (y * weight).astype(jnp.bfloat16)
+            return unused
+
+        lax.fori_loop(0, model // wide, expand, 0)
+
+    def start(copies):
+        for copy in copies:
+            copy.start()
+
+    def arrive(hop, count, onward):
+        for copy in gather(hop):
+            copy.wait_recv()
+        if onward is not None:
+            start(gather(onward))
+        share(hop, count).start()
+        share(hop, count).wait_recv()
+        run_experts(hop, 2 * count)
+        pair(hop, count).start()
+
+    start(gather(1))
+    share(0, rows).start()
+    for load in loads:
+        load.wait()
+    share(0, rows).wait_recv()
+    run_experts(0, 2 * rows)
+    pair(0, rows).start()
+
+    def middle(hop, unused):
+        arrive(hop, 2 * rows, hop + 1)
+        return unused
+
+    lax.fori_loop(1, hops - 1, middle, 0)
+    if hops > 1:
+        arrive(hops - 1, 2 * rows, hops)
+    arrive(hops, rows, None)
+
+    pair(hops, rows).wait_recv()
+    o[hops, :rows] = (
+        o[hops, :rows].astype(jnp.float32) + sibling_sums[hops, :rows].astype(jnp.float32)
+    ).astype(jnp.bfloat16)
+    start(ring(hops))
+
+    def add_up(hop):
+        pair(hop, 2 * rows).wait_recv()
+        for copy in ring(hops if isinstance(hop, int) and hop == hops - 1 else hop + 1):
+            copy.wait_recv()
+        o[hop, : 2 * rows] = (
+            o[hop, : 2 * rows].astype(jnp.float32)
+            + sibling_sums[hop].astype(jnp.float32)
+            + ring_sums[hop].astype(jnp.float32)
+        ).astype(jnp.bfloat16)
+        start(ring(hop))
+
+    if hops > 1:
+        add_up(hops - 1)
+
+    def nearer(i, unused):
+        add_up(hops - 2 - i)
+        return unused
+
+    lax.fori_loop(0, hops - 2, nearer, 0)
+    pair(0, rows).wait_recv()
+    for copy in ring(1):
+        copy.wait_recv()
+    out_ref[...] = (
+        o[0, :rows].astype(jnp.float32)
+        + sibling_sums[0, :rows].astype(jnp.float32)
+        + ring_sums[0, :rows].astype(jnp.float32)
+        + ring_sums[0, rows:].astype(jnp.float32)
+    )
+
+    def sent(hop, count):
+        for copy in gather(hop) + ring(hop) + (share(hop, count), pair(hop, count)):
+            copy.wait_send()
+
+    share(0, rows).wait_send()
+    pair(0, rows).wait_send()
+    if hops > 1:
+        sent(1, 2 * rows)
+
+    def drain(hop, unused):
+        sent(hop, 2 * rows)
+        return unused
+
+    lax.fori_loop(2, hops, drain, 0)
+    sent(hops, rows)
+
+
+def scratch_of(rows, wide, model, ff, devices):
+    hops = devices // 4
+    return [
+        ((hops + 1, 4 * rows, wide), jnp.bfloat16),
+        ((hops + 1, 4 * rows, model), jnp.bfloat16),
+        ((hops + 1, 2 * rows, model), jnp.bfloat16),
+        ((hops, 2 * rows, model), jnp.bfloat16),
+        ((4 * rows, ff), jnp.bfloat16),
+        ((model, ff), jnp.bfloat16),
+        ((model, ff), jnp.bfloat16),
+        ((ff, model), jnp.bfloat16),
+    ]
+
+
+def fits(buffers):
+    return sum(2 * math.prod(shape) for shape, unused in buffers) < 44 * 1024 * 1024
+
+
+def routed_experts(first, w_gate, w_up, w_down, devices):
+    rows, wide = first.shape
+    model, ff = w_gate.shape[1:]
+    hops = devices // 4
+    anywhere = pl.BlockSpec(memory_space=pl.ANY)
+    vmem = pl.BlockSpec(memory_space=pltpu.VMEM)
+    dma = pltpu.SemaphoreType.DMA
+    return pl.pallas_call(
+        functools.partial(experts_kernel, devices),
+        out_shape=jax.ShapeDtypeStruct((rows, model), jnp.float32),
+        in_specs=[vmem, anywhere, anywhere, anywhere],
+        out_specs=vmem,
+        scratch_shapes=[
+            pltpu.VMEM(shape, kind)
+            for shape, kind in scratch_of(rows, wide, model, ff, devices)
+        ]
+        + [dma((3,))]
+        + [dma((2, hops + 1)), dma((2, hops + 1)), dma((hops + 1,)), dma((hops + 1,))]
+        + [dma((hops + 1,)), dma((hops + 1,)), dma((2, hops + 1)), dma((2, hops + 1))],
+        compiler_params=pltpu.CompilerParams(
+            collective_id=0, has_side_effects=True, vmem_limit_bytes=56 * 1024 * 1024
+        ),
+        cost_estimate=pl.CostEstimate(
+            flops=6 * rows * devices * model * ff,
+            bytes_accessed=6 * model * ff,
+            transcendentals=rows * devices * ff,
+        ),
+        name="experts",
+    )(first, w_gate, w_up, w_down)
+
+
 def local(
     query_rows,
     row_key_value,
@@ -165,7 +417,10 @@
     mix = gate_scores / jnp.sum(gate_scores, axis=-1, keepdims=True)
     chosen = expert_ids[..., None] == jnp.arange(experts, dtype=jnp.int32)
     share = jnp.sum(jnp.where(chosen, mix[..., None], 0.0), axis=1)
-    all_share = lax.all_gather(share, "wide", axis=0, tiled=True)
+    high = share.astype(jnp.bfloat16)
+    low = (share - high.astype(jnp.float32)).astype(jnp.bfloat16)
+    spare = -(2 * experts) % LANES
+    shares = jnp.concatenate([high, low, jnp.zeros((rows, spare), jnp.bfloat16)], axis=1)
 
     length = lax.dynamic_slice_in_dim(lengths, doc_index, 1, 0)
     marked = lax.dynamic_index_in_dim(positions, doc_index, 0, keepdims=False)[:, None]
@@ -190,8 +445,20 @@
         * norm_gain
     ).astype(jnp.bfloat16)
 
-    everyone = lax.all_gather(normed, "wide", axis=0, tiled=True)
-    weight = lax.dynamic_slice_in_dim(all_share, device, 1, 1)
+    first = jnp.concatenate([normed, shares], axis=1)
+    model, ff = w_gate.shape[1:]
+    if experts % 4 == 0 and fits(scratch_of(rows, first.shape[1], model, ff, experts)):
+        routed = routed_experts(first, w_gate, w_up, w_down, experts)
+        return (residual + routed).astype(jnp.bfloat16)
+
+    gathered = lax.all_gather(first, "wide", axis=0, tiled=True)
+    everyone = gathered[:, :model]
+    weight = sum(
+        lax.dynamic_slice_in_dim(gathered, model + device + part * experts, 1, 1).astype(
+            jnp.float32
+        )
+        for part in range(2)
+    )
     gate_act = jnp.dot(everyone, w_gate[0], preferred_element_type=jnp.float32)
     up_act = jnp.dot(everyone, w_up[0], preferred_element_type=jnp.float32)
     hidden = (jax.nn.silu(gate_act) * up_act).astype(jnp.bfloat16)

time: 187 us -> 96.4 us (0.52)
  waiting for transfers between devices: 101 us -> 1.45 us
  Pallas kernels: 15.2 us -> 84.1 us
  blocking collectives: 23.5 us -> 0 us
  matrix products: 20.6 us -> 0 us
  between operations: 13.6 us -> 0.09 us
  local copies, waits for them, and re-layouts: 6.88 us -> 4.91 us
    reduce_scatter x1 -> x0, waiting for transfers between devices: 71.3 us -> none  [local(): routed = lax.psum_scatter(weighted, 'wide', scatter_dimension=0, tiled=True)]
    pallas_call x0 -> x1, Pallas kernels: none -> 68.2 us  [routed_experts(): pl.pallas_call(functools.partial(experts_kernel, devices), out_shape=jax....]
    all_gather x1 -> x0, waiting for transfers between devices: 28.3 us -> none  [local(): everyone = lax.all_gather(normed, 'wide', axis=0, tiled=True)]
    all_gather x1 -> x0, blocking collectives: 23.5 us -> none  [local(): all_share = lax.all_gather(share, 'wide', axis=0, tiled=True)]
    dot_general x2 -> x0, matrix products: 20.6 us -> none  [the longest x1 12.3 us: local(): expert_out = jnp.dot(hidden, w_down[0], preferred_element_type=jnp.float32)]
  transfers between devices with their start and end apart: 5 -> 3, of which waited for: 3 -> 1; matrix products, arithmetic and copies ran while one was open for 2% -> 2% of each run, Pallas kernels for 0% -> 0%
where the time goes in v2:
time: 96.4 us; the launch traced here: 96 us
  Pallas kernels  84.1 us (87%)
  local copies, waits for them, and re-layouts  4.91 us (5%)
  other arithmetic  4.37 us (5%)
  waiting for transfers between devices  1.45 us (2%)
  starting transfers between devices  1.09 us (1%)
    pallas_call x1, Pallas kernels, routed_experts(): pl.pallas_call(functools.partial(experts_kernel, devices), out_shape=jax....  68.2 us
    pallas_call x1, Pallas kernels, attention(): pl.pallas_call(attention_kernel, out_shape=(jax.ShapeDtypeStruct((pairs,...  15.9 us
    unnamed x14, local copies, waits for them, and re-layouts  2.45 us
    convert_element_type x1, other arithmetic, local(): return (residual + routed).astype(jnp.bfloat16)  2 us
  transfers between devices with their start and end apart: 3, of which 1 were waited for; matrix products, arithmetic and copies ran while one was open for 2% of the time, Pallas kernels for 0%

profile of v2, /device:TPU:0, one launch (start us, length us, event | category | flops | bytes accessed | tf_op | source)
XLA Modules:
  0.0 96.0 jit_solution(8533141658065018129)
XLA Ops:
  0.0 0.0 copy-start
  0.0 0.5 collective-permute-start
  0.5 1.3 %dynamic_slice.7.length_ref = s32[1]{0:T(128)} dynamic-slice(s32[8]{0:T(128)} %param.17, s32[]{:T(128)S(6)} %select_n.22), dynamic_slice_sizes={1} | dynamic-slice | bytes 12 | tf_op jit(solution)/shard_map/dynamic_slice | solution.py:425
  1.8 0.0 copy-done
  1.8 0.1 copy.21.marked_ref
  1.9 0.7 reduce_sum.28
  2.6 0.0 collective-permute-done
  2.6 1.0 %pad_maximum_fusion.q_ref = bf16[128,2048]{1,0:T(8,128)(2,1)S(1)} fusion(bf16[64,2048]{1,0:T(8,128)(2,1)S(1)} %collective-permute-done, bf16[64,2048]{1,0:T(8,128)(2,1)} %param.12), kind=kLoop, calls=%fused_computation.5 | loop fusion | flops 1048576 | bytes 1048576 | tf_op jit(solution)/shard_map/concatenate | solution.py:430
  3.6 0.0 copy-start.1
  3.6 1.6 %copy-done.1 = bf16[2048,512]{1,0:T(8,128)(2,1)S(1)} copy-done((bf16[2048,512]{1,0:T(8,128)(2,1)S(1)}, bf16[2048,512]{1,0:T(8,128)(2,1)}, u32[]{:S(2)}) %copy-start.1) | copy-done | bytes 2097176
  5.2 0.0 copy-start.2
  5.2 0.8 copy-done.2
  6.0 0.0 copy-start.4
  6.0 0.0 copy-start.6
  6.0 0.0 copy-start.3
  6.0 15.9 %attention.1 = (bf16[16,128,128]{2,1,0:T(8,128)(2,1)S(1)}, f32[16,128,128]{2,1,0:T(8,128)S(1)}) custom-call(s32[1]{0:T(128)} %bitcast.start_ref, s32[1]{0:T(128)} %dynamic_slice.7.length_ref, bf16[128,2048]{1,0:T(8,128)(2,1)S(1)} %pad_maximum_fusion.q_ref, bf16[2048,512]{1,0:T(8,128)(2,1)S(1)} %copy-done.1, bf16[64,512]{1,0:T(8,128)(2,1)S(1)} %copy-done.2, ...), custom_call_target="tpu_custom_call" | custom-call | flops 2281701376 | bytes 4194304 | tf_op jit(solution)/shard_map/attention/pallas_call | solution.py:119
  22.0 0.0 copy-start.5
  22.0 0.1 collective-permute-start.2
  22.2 0.0 copy-done.4
  22.2 0.5 collective-permute-start.1
  22.7 0.0 copy-done.6
  22.7 0.1 copy.24
  22.8 0.1 copy.25
  22.9 1.4 %collective-permute-done.1 = bf16[16,64,128]{2,1,0:T(8,128)(2,1)S(1)} collective-permute-done((bf16[16,64,128]{2,1,0:T(8,128)(2,1)S(1)}, bf16[16,64,128]{2,1,0:T(8,128)(2,1)S(1)}, u32[]{:S(2)}, u32[]{:S(2)}) %collective-permute-start.1) | collective-permute-done | bytes 262176 | tf_op jit(solution)/shard_map/ppermute | solution.py:18
  24.4 0.0 collective-permute-done.2
  24.4 0.0 copy-done.3
  24.4 0.3 multiply_reduce_fusion
  24.7 0.0 copy-done.5
  24.8 0.3 multiply_convert_fusion
  25.0 0.8 concatenate.7.first_ref
  25.8 68.2 %experts.1 = f32[64,2048]{1,0:T(8,128)} custom-call(bf16[64,2176]{1,0:T(8,128)(2,1)} %concatenate.7.first_ref, bf16[1,2048,768]{2,1,0:T(8,128)(2,1)} %gate_hbm.1, bf16[1,2048,768]{2,1,0:T(8,128)(2,1)} %up_hbm.1, bf16[1,768,2048]{2,1,0:T(8,128)(2,1)} %down_hbm.1), custom_call_target="tpu_custom_call" | custom-call | flops 9663676416 | bytes 9437184 | tf_op jit(solution)/shard_map/experts/pallas_call | solution.py:371
  94.0 2.0 %add_convert_fusion = bf16[64,2048]{1,0:T(8,128)(2,1)} fusion(f32[64,2048]{1,0:T(8,128)} %experts.1, bf16[64,2048]{1,0:T(8,128)(2,1)S(1)} %copy-done.3, f32[16,64,128]{2,1,0:T(8,128)S(1)} %collective-permute-done.2, f32[16,128,128]{2,1,0:T(8,128)S(1)} %get-tuple-element.8, bf16[16,64,128]{2,1,0:T(8,128)(2,1)S(1)} %collective-permute-done.1, ...), kind=kLoop, calls=%fused_computation.7 | loop fusion | flops 1835008 | bytes 2621440 | tf_op jit(solution)/shard_map/convert_element_type | solution.py:452
  (9 shorter events, 0.1 us)
Async XLA Ops:
  0.0 1.8 %copy-start = (s32[8,128]{1,0:T(8,128)S(1)}, s32[8,128]{1,0:T(8,128)}, u32[]{:S(2)}) copy-start(s32[8,128]{1,0:T(8,128)} %param.18) | copy-start | bytes 12292
  0.0 2.6 %collective-permute-start = (bf16[64,2048]{1,0:T(8,128)(2,1)}, bf16[64,2048]{1,0:T(8,128)(2,1)S(1)}, u32[]{:S(2)}, u32[]{:S(2)}) collective-permute-start(bf16[64,2048]{1,0:T(8,128)(2,1)} %param.12), channel_id=1, source_target_pairs={{0,1},{1,0},{2,3},{3,2},{4,5},{5,4},{6,7},{7,6},{8,9},{9,8},{10,11... | collective-permute-start | bytes 786440 | tf_op jit(solution)/shard_map/ppermute | solution.py:18
  3.6 1.6 %copy-start.1 = (bf16[2048,512]{1,0:T(8,128)(2,1)S(1)}, bf16[2048,512]{1,0:T(8,128)(2,1)}, u32[]{:S(2)}) copy-start(bf16[2048,512]{1,0:T(8,128)(2,1)} %cache_ref.1) | copy-start | bytes 6291460
  5.2 0.8 copy-start.2
  6.0 16.1 %copy-start.4 = (f32[64,8]{0,1:T(8,128)S(1)}, f32[64,8]{0,1:T(8,128)}, u32[]{:S(2)}) copy-start(f32[64,8]{0,1:T(8,128)} %param.20) | copy-start | bytes 6148
  6.0 16.7 %copy-start.6 = (s32[64,8]{0,1:T(8,128)S(1)}, s32[64,8]{0,1:T(8,128)}, u32[]{:S(2)}) copy-start(s32[64,8]{0,1:T(8,128)} %param.19) | copy-start | bytes 6148
  6.0 18.3 %copy-start.3 = (bf16[64,2048]{1,0:T(8,128)(2,1)S(1)}, bf16[64,2048]{1,0:T(8,128)(2,1)}, u32[]{:S(2)}) copy-start(bf16[64,2048]{1,0:T(8,128)(2,1)} %param.15) | copy-start | bytes 786436
  22.0 2.8 %copy-start.5 = (f32[2048]{0:T(1024)S(1)}, f32[2048]{0:T(1024)}, u32[]{:S(2)}) copy-start(f32[2048]{0:T(1024)} %param.16) | copy-start | bytes 24580
  22.0 2.4 %collective-permute-start.2 = (f32[16,64,128]{2,1,0:T(8,128)S(1)}, f32[16,64,128]{2,1,0:T(8,128)S(1)}, u32[]{:S(2)}, u32[]{:S(2)}) collective-permute-start(f32[16,64,128]{2,1,0:T(8,128)S(1)} %slice.15), channel_id=1, source_target_pairs={{0,1},{1,0},{2,3},{3,2},{4,5},{5,4},{6,7},{7,6},{8,9},{9,8},{10,11... | collective-permute-start | bytes 1572872 | tf_op jit(solution)/shard_map/ppermute | solution.py:18
  22.2 2.2 %collective-permute-start.1 = (bf16[16,64,128]{2,1,0:T(8,128)(2,1)S(1)}, bf16[16,64,128]{2,1,0:T(8,128)(2,1)S(1)}, u32[]{:S(2)}, u32[]{:S(2)}) collective-permute-start(bf16[16,64,128]{2,1,0:T(8,128)(2,1)S(1)} %slice.13), channel_id=1, source_target_pairs={{0,1},{1,0},{2,3},{3,2},{4,5},{5,4},{6,7},{7,6},{8,9},{9,8},{10,11... | collective-permute-start | bytes 786440 | tf_op jit(solution)/shard_map/ppermute | solution.py:18

commit v3 on v2

--- a/solution.py
+++ b/solution.py
@@ -172,6 +172,9 @@
             device_id={"wide": device}, device_id_type=pl.DeviceIdType.MESH,
         )
 
+    parts = (pl.ds(0, model // 2), pl.ds(model // 2, model // 2))
+    wide_parts = (pl.ds(0, model // 2), pl.ds(model // 2, x.shape[2] - model // 2))
+
     loads = [
         pltpu.make_async_copy(source.at[0], target, weight_sem.at[i])
         for i, (source, target) in enumerate(
@@ -190,7 +193,7 @@
         )
     pl.semaphore_wait(barrier, 3)
 
-    def gather(hop):
+    def gather(hop, part):
         if isinstance(hop, int) and hop == hops:
             top, bottom = pl.ds(0, half), pl.ds(half, half)
             from_left, from_right = top, bottom if hop == 1 else pl.ds(rows + half, half)
@@ -201,33 +204,37 @@
                 from_right = pl.ds(0, rows)
         to_left = pl.ds(0, rows) if top is None else top
         to_right = pl.ds(rows, rows) if bottom is None else bottom
+        columns = wide_parts[part]
         return (
-            remote(x.at[hop - 1, from_left], x.at[hop, to_left],
-                   gather_send.at[0, hop], gather_recv.at[0, hop], right),
-            remote(x.at[hop - 1, from_right], x.at[hop, to_right],
-                   gather_send.at[1, hop], gather_recv.at[1, hop], left),
-        )
-
-    def share(hop, count):
-        return remote(x.at[hop, pl.ds(0, count)], x.at[hop, pl.ds(count, count)],
-                      share_send.at[hop], share_recv.at[hop], sibling)
-
-    def pair(hop, count):
-        return remote(o.at[hop, pl.ds(count, count)], sibling_sums.at[hop, pl.ds(0, count)],
-                      pair_send.at[hop], pair_recv.at[hop], sibling)
-
-    def ring(hop):
+            remote(x.at[hop - 1, from_left, columns], x.at[hop, to_left, columns],
+                   gather_send.at[0, part, hop], gather_recv.at[0, part, hop], right),
+            remote(x.at[hop - 1, from_right, columns], x.at[hop, to_right, columns],
+                   gather_send.at[1, part, hop], gather_recv.at[1, part, hop], left),
+        )
+
+    def share(hop, count, part):
+        return remote(x.at[hop, pl.ds(0, count), wide_parts[part]],
+                      x.at[hop, pl.ds(count, count), wide_parts[part]],
+                      share_send.at[part, hop], share_recv.at[part, hop], sibling)
+
+    def pair(hop, count, part):
+        return remote(o.at[hop, pl.ds(count, count), parts[part]],
+                      sibling_sums.at[hop, pl.ds(0, count), parts[part]],
+                      pair_send.at[part, hop], pair_recv.at[part, hop], sibling)
+
+    def ring(hop, part):
         if isinstance(hop, int) and hop == hops:
             go_left = land_left = pl.ds(0, half)
             go_right, land_right = pl.ds(half, half), pl.ds(rows + half, half)
         else:
             go_left = land_left = pl.ds(0, rows)
             go_right = land_right = pl.ds(rows, rows)
+        columns = parts[part]
         return (
-            remote(o.at[hop, go_left], ring_sums.at[hop - 1, land_left],
-                   ring_send.at[0, hop], ring_recv.at[0, hop], left),
-            remote(o.at[hop, go_right], ring_sums.at[hop - 1, land_right],
-                   ring_send.at[1, hop], ring_recv.at[1, hop], right),
+            remote(o.at[hop, go_left, columns], ring_sums.at[hop - 1, land_left, columns],
+                   ring_send.at[0, part, hop], ring_recv.at[0, part, hop], left),
+            remote(o.at[hop, go_right, columns], ring_sums.at[hop - 1, land_right, columns],
+                   ring_send.at[1, part, hop], ring_recv.at[1, part, hop], right),
         )
 
     def chunk_of(size):
@@ -249,38 +256,46 @@
             hidden[:count, columns] = (g / (1.0 + jnp.exp(-g)) * u).astype(jnp.bfloat16)
             return unused
 
-        lax.fori_loop(0, ff // step, hide, 0)
-        wide = chunk_of(model)
-
-        def expand(i, unused):
-            columns = pl.ds(pl.multiple_of(i * wide, wide), wide)
-            y = jnp.dot(hidden[:count], w_down[:, columns], preferred_element_type=jnp.float32)
-            o[hop, :count, columns] = (y * weight).astype(jnp.bfloat16)
-            return unused
-
-        lax.fori_loop(0, model // wide, expand, 0)
-
-    def start(copies):
-        for copy in copies:
+        lax.fori_loop(0, ff // step, hide, 0, unroll=True)
+        wide = chunk_of(model // 2)
+
+        for part in range(2):
+
+            def expand(i, unused):
+                first_column = part * (model // 2) + i * wide
+                columns = pl.ds(pl.multiple_of(first_column, wide), wide)
+                y = jnp.dot(
+                    hidden[:count], w_down[:, columns], preferred_element_type=jnp.float32
+                )
+                o[hop, :count, columns] = (y * weight).astype(jnp.bfloat16)
+                return unused
+
+            lax.fori_loop(0, model // 2 // wide, expand, 0, unroll=True)
+            pair(hop, count // 2, part).start()
+
+    def arrive(hop, count, onward):
+        for part in range(2):
+            coming = gather(hop, part)
+            going = (None, None) if onward is None else gather(onward, part)
+            for come, go in zip(coming, going):
+                come.wait_recv()
+                if go is not None:
+                    go.start()
+            share(hop, count, part).start()
+        for part in range(2):
+            share(hop, count, part).wait_recv()
+        run_experts(hop, 2 * count)
+
+    for part in range(2):
+        for copy in gather(1, part):
             copy.start()
-
-    def arrive(hop, count, onward):
-        for copy in gather(hop):
-            copy.wait_recv()
-        if onward is not None:
-            start(gather(onward))
-        share(hop, count).start()
-        share(hop, count).wait_recv()
-        run_experts(hop, 2 * count)
-        pair(hop, count).start()
-
-    start(gather(1))
-    share(0, rows).start()
+    for part in range(2):
+        share(0, rows, part).start()
     for load in loads:
         load.wait()
-    share(0, rows).wait_recv()
+    for part in range(2):
+        share(0, rows, part).wait_recv()
     run_experts(0, 2 * rows)
-    pair(0, rows).start()
 
     def middle(hop, unused):
         arrive(hop, 2 * rows, hop + 1)
@@ -291,22 +306,31 @@
         arrive(hops - 1, 2 * rows, hops)
     arrive(hops, rows, None)
 
-    pair(hops, rows).wait_recv()
-    o[hops, :rows] = (
-        o[hops, :rows].astype(jnp.float32) + sibling_sums[hops, :rows].astype(jnp.float32)
-    ).astype(jnp.bfloat16)
-    start(ring(hops))
+    def wider(ref, hop, some, columns):
+        return ref[hop, some, columns].astype(jnp.float32)
+
+    for part, columns in enumerate(parts):
+        pair(hops, rows, part).wait_recv()
+        some = pl.ds(0, rows)
+        o[hops, some, columns] = (
+            wider(o, hops, some, columns) + wider(sibling_sums, hops, some, columns)
+        ).astype(jnp.bfloat16)
+        for copy in ring(hops, part):
+            copy.start()
 
     def add_up(hop):
-        pair(hop, 2 * rows).wait_recv()
-        for copy in ring(hops if isinstance(hop, int) and hop == hops - 1 else hop + 1):
-            copy.wait_recv()
-        o[hop, : 2 * rows] = (
-            o[hop, : 2 * rows].astype(jnp.float32)
-            + sibling_sums[hop].astype(jnp.float32)
-            + ring_sums[hop].astype(jnp.float32)
-        ).astype(jnp.bfloat16)
-        start(ring(hop))
+        further = hops if isinstance(hop, int) and hop == hops - 1 else hop + 1
+        for part, columns in enumerate(parts):
+            pair(hop, 2 * rows, part).wait_recv()
+            for side, (come, go) in enumerate(zip(ring(further, part), ring(hop, part))):
+                come.wait_recv()
+                some = pl.ds(side * rows, rows)
+                o[hop, some, columns] = (
+                    wider(o, hop, some, columns)
+                    + wider(sibling_sums, hop, some, columns)
+                    + wider(ring_sums, hop, some, columns)
+                ).astype(jnp.bfloat16)
+                go.start()
 
     if hops > 1:
         add_up(hops - 1)
@@ -316,22 +340,28 @@
         return unused
 
     lax.fori_loop(0, hops - 2, nearer, 0)
-    pair(0, rows).wait_recv()
-    for copy in ring(1):
-        copy.wait_recv()
-    out_ref[...] = (
-        o[0, :rows].astype(jnp.float32)
-        + sibling_sums[0, :rows].astype(jnp.float32)
-        + ring_sums[0, :rows].astype(jnp.float32)
-        + ring_sums[0, rows:].astype(jnp.float32)
-    )
+    for part, columns in enumerate(parts):
+        pair(0, rows, part).wait_recv()
+        for copy in ring(1, part):
+            copy.wait_recv()
+        some, rest = pl.ds(0, rows), pl.ds(rows, rows)
+        out_ref[:, columns] = (
+            wider(o, 0, some, columns)
+            + wider(sibling_sums, 0, some, columns)
+            + wider(ring_sums, 0, some, columns)
+            + wider(ring_sums, 0, rest, columns)
+        )
 
     def sent(hop, count):
-        for copy in gather(hop) + ring(hop) + (share(hop, count), pair(hop, count)):
-            copy.wait_send()
-
-    share(0, rows).wait_send()
-    pair(0, rows).wait_send()
+        for part in range(2):
+            for copy in gather(hop, part) + ring(hop, part):
+                copy.wait_send()
+            share(hop, count, part).wait_send()
+            pair(hop, count, part).wait_send()
+
+    for part in range(2):
+        share(0, rows, part).wait_send()
+        pair(0, rows, part).wait_send()
     if hops > 1:
         sent(1, 2 * rows)
 
@@ -378,8 +408,8 @@
             for shape, kind in scratch_of(rows, wide, model, ff, devices)
         ]
         + [dma((3,))]
-        + [dma((2, hops + 1)), dma((2, hops + 1)), dma((hops + 1,)), dma((hops + 1,))]
-        + [dma((hops + 1,)), dma((hops + 1,)), dma((2, hops + 1)), dma((2, hops + 1))],
+        + [dma((2, 2, hops + 1)), dma((2, 2, hops + 1)), dma((2, hops + 1)), dma((2, hops + 1))]
+        + [dma((2, hops + 1)), dma((2, hops + 1)), dma((2, 2, hops + 1)), dma((2, 2, hops + 1))],
         compiler_params=pltpu.CompilerParams(
             collective_id=0, has_side_effects=True, vmem_limit_bytes=56 * 1024 * 1024
         ),

time: 96.4 us -> 85.3 us (0.88)
  Pallas kernels: 84.1 us -> 73 us
    pallas_call x1, Pallas kernels: 68.2 us -> 57.1 us  [routed_experts(): pl.pallas_call(functools.partial(experts_kernel, devices), out_shape=jax....]
  transfers between devices with their start and end apart: 3 -> 3, of which waited for: 1 -> 1; matrix products, arithmetic and copies ran while one was open for 2% -> 3% of each run, Pallas kernels for 0% -> 0%
where the time goes in v3:
time: 85.3 us; the launch traced here: 84.9 us
  Pallas kernels  73 us (86%)
  local copies, waits for them, and re-layouts  4.91 us (6%)
  other arithmetic  4.37 us (5%)
  waiting for transfers between devices  1.45 us (2%)
  starting transfers between devices  1.09 us (1%)
    pallas_call x1, Pallas kernels, routed_experts(): pl.pallas_call(functools.partial(experts_kernel, devices), out_shape=jax....  57.1 us
    pallas_call x1, Pallas kernels, attention(): pl.pallas_call(attention_kernel, out_shape=(jax.ShapeDtypeStruct((pairs,...  15.9 us
    unnamed x14, local copies, waits for them, and re-layouts  2.45 us
    convert_element_type x1, other arithmetic, local(): return (residual + routed).astype(jnp.bfloat16)  2 us
  transfers between devices with their start and end apart: 3, of which 1 were waited for; matrix products, arithmetic and copies ran while one was open for 3% of the time, Pallas kernels for 0%

profile of v3, /device:TPU:0, one launch (start us, length us, event | category | flops | bytes accessed | tf_op | source)
XLA Modules:
  0.0 84.9 jit_solution(933616942015897068)
XLA Ops:
  0.0 0.0 copy-start
  0.0 0.5 collective-permute-start
  0.5 1.3 %dynamic_slice.7.length_ref = s32[1]{0:T(128)} dynamic-slice(s32[8]{0:T(128)} %param.17, s32[]{:T(128)S(6)} %select_n.22), dynamic_slice_sizes={1} | dynamic-slice | bytes 12 | tf_op jit(solution)/shard_map/dynamic_slice | solution.py:455
  1.8 0.0 copy-done
  1.8 0.1 copy.21.marked_ref
  1.9 0.7 reduce_sum.28
  2.6 0.0 collective-permute-done
  2.6 1.0 %pad_maximum_fusion.q_ref = bf16[128,2048]{1,0:T(8,128)(2,1)S(1)} fusion(bf16[64,2048]{1,0:T(8,128)(2,1)S(1)} %collective-permute-done, bf16[64,2048]{1,0:T(8,128)(2,1)} %param.12), kind=kLoop, calls=%fused_computation.5 | loop fusion | flops 1048576 | bytes 1048576 | tf_op jit(solution)/shard_map/concatenate | solution.py:460
  3.6 0.0 copy-start.1
  3.6 1.6 %copy-done.1 = bf16[2048,512]{1,0:T(8,128)(2,1)S(1)} copy-done((bf16[2048,512]{1,0:T(8,128)(2,1)S(1)}, bf16[2048,512]{1,0:T(8,128)(2,1)}, u32[]{:S(2)}) %copy-start.1) | copy-done | bytes 2097176
  5.2 0.0 copy-start.2
  5.2 0.8 copy-done.2
  6.0 0.0 copy-start.4
  6.0 0.0 copy-start.6
  6.0 0.0 copy-start.3
  6.0 15.9 %attention.1 = (bf16[16,128,128]{2,1,0:T(8,128)(2,1)S(1)}, f32[16,128,128]{2,1,0:T(8,128)S(1)}) custom-call(s32[1]{0:T(128)} %bitcast.start_ref, s32[1]{0:T(128)} %dynamic_slice.7.length_ref, bf16[128,2048]{1,0:T(8,128)(2,1)S(1)} %pad_maximum_fusion.q_ref, bf16[2048,512]{1,0:T(8,128)(2,1)S(1)} %copy-done.1, bf16[64,512]{1,0:T(8,128)(2,1)S(1)} %copy-done.2, ...), custom_call_target="tpu_custom_call" | custom-call | flops 2281701376 | bytes 4194304 | tf_op jit(solution)/shard_map/attention/pallas_call | solution.py:119
  22.0 0.0 copy-start.5
  22.0 0.1 collective-permute-start.2
  22.2 0.0 copy-done.4
  22.2 0.5 collective-permute-start.1
  22.7 0.0 copy-done.6
  22.7 0.1 copy.24
  22.8 0.1 copy.25
  22.9 1.4 %collective-permute-done.1 = bf16[16,64,128]{2,1,0:T(8,128)(2,1)S(1)} collective-permute-done((bf16[16,64,128]{2,1,0:T(8,128)(2,1)S(1)}, bf16[16,64,128]{2,1,0:T(8,128)(2,1)S(1)}, u32[]{:S(2)}, u32[]{:S(2)}) %collective-permute-start.1) | collective-permute-done | bytes 262176 | tf_op jit(solution)/shard_map/ppermute | solution.py:18
  24.4 0.0 collective-permute-done.2
  24.4 0.0 copy-done.3
  24.4 0.3 multiply_reduce_fusion
  24.7 0.0 copy-done.5
  24.8 0.3 multiply_convert_fusion
  25.0 0.8 concatenate.7.first_ref
  25.8 57.1 %experts.1 = f32[64,2048]{1,0:T(8,128)} custom-call(bf16[64,2176]{1,0:T(8,128)(2,1)} %concatenate.7.first_ref, bf16[1,2048,768]{2,1,0:T(8,128)(2,1)} %gate_hbm.1, bf16[1,2048,768]{2,1,0:T(8,128)(2,1)} %up_hbm.1, bf16[1,768,2048]{2,1,0:T(8,128)(2,1)} %down_hbm.1), custom_call_target="tpu_custom_call" | custom-call | flops 9663676416 | bytes 9437184 | tf_op jit(solution)/shard_map/experts/pallas_call | solution.py:401
  82.9 2.0 %add_convert_fusion = bf16[64,2048]{1,0:T(8,128)(2,1)} fusion(f32[64,2048]{1,0:T(8,128)} %experts.1, bf16[64,2048]{1,0:T(8,128)(2,1)S(1)} %copy-done.3, f32[16,64,128]{2,1,0:T(8,128)S(1)} %collective-permute-done.2, f32[16,128,128]{2,1,0:T(8,128)S(1)} %get-tuple-element.8, bf16[16,64,128]{2,1,0:T(8,128)(2,1)S(1)} %collective-permute-done.1, ...), kind=kLoop, calls=%fused_computation.7 | loop fusion | flops 1835008 | bytes 2621440 | tf_op jit(solution)/shard_map/convert_element_type | solution.py:482
  (9 shorter events, 0.1 us)
Async XLA Ops:
  0.0 1.8 %copy-start = (s32[8,128]{1,0:T(8,128)S(1)}, s32[8,128]{1,0:T(8,128)}, u32[]{:S(2)}) copy-start(s32[8,128]{1,0:T(8,128)} %param.18) | copy-start | bytes 12292
  0.0 2.6 %collective-permute-start = (bf16[64,2048]{1,0:T(8,128)(2,1)}, bf16[64,2048]{1,0:T(8,128)(2,1)S(1)}, u32[]{:S(2)}, u32[]{:S(2)}) collective-permute-start(bf16[64,2048]{1,0:T(8,128)(2,1)} %param.12), channel_id=1, source_target_pairs={{0,1},{1,0},{2,3},{3,2},{4,5},{5,4},{6,7},{7,6},{8,9},{9,8},{10,11... | collective-permute-start | bytes 786440 | tf_op jit(solution)/shard_map/ppermute | solution.py:18
  3.6 1.6 %copy-start.1 = (bf16[2048,512]{1,0:T(8,128)(2,1)S(1)}, bf16[2048,512]{1,0:T(8,128)(2,1)}, u32[]{:S(2)}) copy-start(bf16[2048,512]{1,0:T(8,128)(2,1)} %cache_ref.1) | copy-start | bytes 6291460
  5.2 0.8 copy-start.2
  6.0 16.1 %copy-start.4 = (f32[64,8]{0,1:T(8,128)S(1)}, f32[64,8]{0,1:T(8,128)}, u32[]{:S(2)}) copy-start(f32[64,8]{0,1:T(8,128)} %param.20) | copy-start | bytes 6148
  6.0 16.7 %copy-start.6 = (s32[64,8]{0,1:T(8,128)S(1)}, s32[64,8]{0,1:T(8,128)}, u32[]{:S(2)}) copy-start(s32[64,8]{0,1:T(8,128)} %param.19) | copy-start | bytes 6148
  6.0 18.3 %copy-start.3 = (bf16[64,2048]{1,0:T(8,128)(2,1)S(1)}, bf16[64,2048]{1,0:T(8,128)(2,1)}, u32[]{:S(2)}) copy-start(bf16[64,2048]{1,0:T(8,128)(2,1)} %param.15) | copy-start | bytes 786436
  22.0 2.8 %copy-start.5 = (f32[2048]{0:T(1024)S(1)}, f32[2048]{0:T(1024)}, u32[]{:S(2)}) copy-start(f32[2048]{0:T(1024)} %param.16) | copy-start | bytes 24580
  22.0 2.4 %collective-permute-start.2 = (f32[16,64,128]{2,1,0:T(8,128)S(1)}, f32[16,64,128]{2,1,0:T(8,128)S(1)}, u32[]{:S(2)}, u32[]{:S(2)}) collective-permute-start(f32[16,64,128]{2,1,0:T(8,128)S(1)} %slice.15), channel_id=1, source_target_pairs={{0,1},{1,0},{2,3},{3,2},{4,5},{5,4},{6,7},{7,6},{8,9},{9,8},{10,11... | collective-permute-start | bytes 1572872 | tf_op jit(solution)/shard_map/ppermute | solution.py:18
  22.2 2.2 %collective-permute-start.1 = (bf16[16,64,128]{2,1,0:T(8,128)(2,1)S(1)}, bf16[16,64,128]{2,1,0:T(8,128)(2,1)S(1)}, u32[]{:S(2)}, u32[]{:S(2)}) collective-permute-start(bf16[16,64,128]{2,1,0:T(8,128)(2,1)S(1)} %slice.13), channel_id=1, source_target_pairs={{0,1},{1,0},{2,3},{3,2},{4,5},{5,4},{6,7},{7,6},{8,9},{9,8},{10,11... | collective-permute-start | bytes 786440 | tf_op jit(solution)/shard_map/ppermute | solution.py:18

commit v4 on v3

--- a/solution.py
+++ b/solution.py
@@ -32,17 +32,11 @@
     ).astype(jnp.bfloat16)
 
 
-def attention_kernel(
-    start_ref, length_ref, q_ref, cache_ref, rows_ref, marked_ref, out_ref, lse_ref,
-    q_scr, k_scr, v_scr, s_scr,
-):
-    rows = q_ref.shape[0]
+def place_keys(start_ref, length_ref, cache_ref, rows_ref, marked_ref, k_scr, v_scr):
     span = cache_ref.shape[0]
     own = rows_ref.shape[0]
     keys = k_scr.shape[2]
-    query_heads = q_ref.shape[1] // HEAD_SIZE
     width = KEY_VALUE_HEADS * HEAD_SIZE
-    group = query_heads // KEY_VALUE_HEADS
 
     location = lane_index((1, keys))
     place = start_ref[0] + location
@@ -70,21 +64,31 @@
             k_scr[head, :HEAD_SIZE, :] = slab_keys[odd * HEAD_SIZE : (odd + 1) * HEAD_SIZE, :]
             k_scr[head, HEAD_SIZE:, :] = bias_rows
             v_scr[head] = half_with_one(slab_values, odd)
-    for pair in range(query_heads // 2):
+
+
+def place_queries(q_ref, q_scr, first):
+    rows = q_ref.shape[0]
+    stride = q_scr.shape[1] // 2
+    for pair in range(q_scr.shape[0]):
         slab = q_ref[:, pair * LANES : (pair + 1) * LANES].astype(jnp.float32) * (
             1.0 / math.sqrt(HEAD_SIZE)
         )
         for odd in range(2):
-            q_scr[pair, odd * rows : (odd + 1) * rows, :] = half_with_one(slab, odd)
-
-    pairs = query_heads // 2
+            at = odd * stride + first
+            q_scr[pair, at : at + rows, :] = half_with_one(slab, odd)
+
+
+def attend(q_scr, k_scr, v_scr, s_scr, store, after_step):
+    pairs = q_scr.shape[0]
+    rows = q_scr.shape[1] // 2
+    group = pairs // KEY_VALUE_HEADS
 
     def scores(pair, slot):
-        head = lax.div(pair, group // 2)
+        head = lax.div(pair, group)
         s_scr[slot] = jnp.dot(q_scr[pair], k_scr[head], preferred_element_type=jnp.float32)
 
     def finish(pair, slot):
-        head = lax.div(pair, group // 2)
+        head = lax.div(pair, group)
         s = s_scr[slot]
         largest = jnp.max(s, axis=1, keepdims=True)
         p = jnp.exp(s - largest).astype(jnp.bfloat16)
@@ -93,10 +97,11 @@
         mean = summed / total
         lse = jnp.broadcast_to(largest + jnp.log(total), mean.shape)
         low = lane_index((rows, LANES)) < HEAD_SIZE
-        out_ref[pair] = jnp.where(
-            low, mean[:rows], pltpu.roll(mean[rows:], HEAD_SIZE, 1)
-        ).astype(jnp.bfloat16)
-        lse_ref[pair] = jnp.where(low, lse[:rows], lse[rows:])
+        store(
+            pair,
+            jnp.where(low, mean[:rows], pltpu.roll(mean[rows:], HEAD_SIZE, 1)),
+            jnp.where(low, lse[:rows], lse[rows:]),
+        )
 
     scores(0, 0)
 
@@ -105,9 +110,24 @@
         finish(2 * j, 0)
         scores(jnp.minimum(2 * j + 2, pairs - 1), 0)
         finish(2 * j + 1, 1)
+        after_step(j)
         return unused
 
     lax.fori_loop(0, pairs // 2, step, 0)
+
+
+def attention_kernel(
+    start_ref, length_ref, q_ref, cache_ref, rows_ref, marked_ref, out_ref, lse_ref,
+    q_scr, k_scr, v_scr, s_scr,
+):
+    place_keys(start_ref, length_ref, cache_ref, rows_ref, marked_ref, k_scr, v_scr)
+    place_queries(q_ref, q_scr, 0)
+
+    def store(pair, mean, lse):
+        out_ref[pair] = mean.astype(jnp.bfloat16)
+        lse_ref[pair] = lse
+
+    attend(q_scr, k_scr, v_scr, s_scr, store, lambda j: None)
 
 
 def attention(queries, cache, row_key_value, start, length, marked):
@@ -149,12 +169,16 @@
 
 
 def experts_kernel(
-    devices, first_ref, gate_hbm, up_hbm, down_hbm, out_ref,
+    devices, start_ref, length_ref, q_ref, cache_ref, rows_ref, marked_ref,
+    resid_ref, gain_ref, shares_ref, gate_hbm, up_hbm, down_hbm, out_ref,
+    q_scr, k_scr, v_scr, s_scr, visitor, own_mean, own_lse, host_mean, host_lse,
+    far_mean, far_lse, residual,
+    visit_sem, mean_send, mean_recv, lse_send, lse_recv,
     x, o, sibling_sums, ring_sums, hidden, w_gate, w_up, w_down,
     weight_sem, gather_send, gather_recv, share_send, share_recv,
     pair_send, pair_recv, ring_send, ring_recv,
 ):
-    rows, half = first_ref.shape[0], first_ref.shape[0] // 2
+    rows, half = q_ref.shape[0], q_ref.shape[0] // 2
     model = out_ref.shape[1]
     ff = w_down.shape[0]
     chips = devices // 2
@@ -183,7 +207,7 @@
     ]
     for load in loads:
         load.start()
-    x[0, :rows] = first_ref[...]
+    x[0, :rows, model:] = shares_ref[...]
     ring_sums[hops - 1, half : rows + half] = jnp.zeros((rows, model), jnp.bfloat16)
 
     barrier = pltpu.get_barrier_semaphore()
@@ -192,6 +216,52 @@
             barrier, inc=1, device_id={"wide": neighbour}, device_id_type=pl.DeviceIdType.MESH
         )
     pl.semaphore_wait(barrier, 3)
+
+    visit = remote(q_ref, visitor, visit_sem.at[0], visit_sem.at[1], sibling)
+    visit.start()
+    place_keys(start_ref, length_ref, cache_ref, rows_ref, marked_ref, k_scr, v_scr)
+    place_queries(q_ref, q_scr, 0)
+    visit.wait_recv()
+    place_queries(visitor, q_scr, rows)
+
+    def store(pair, mean, lse):
+        own_mean[pair] = mean[:rows]
+        own_lse[pair] = lse[:rows]
+        host_mean[pair] = mean[rows:].astype(jnp.bfloat16)
+        host_lse[pair] = lse[rows:]
+
+    def returned(j):
+        two = pl.ds(2 * j, 2)
+        return (
+            remote(host_mean.at[two], far_mean.at[two], mean_send.at[j], mean_recv.at[j], sibling),
+            remote(host_lse.at[two], far_lse.at[two], lse_send.at[j], lse_recv.at[j], sibling),
+        )
+
+    def send_back(j):
+        for copy in returned(j):
+            copy.start()
+
+    attend(q_scr, k_scr, v_scr, s_scr, store, send_back)
+
+    pairs = q_scr.shape[0]
+    squares = jnp.zeros((rows, LANES), jnp.float32)
+    for pair in range(pairs):
+        if pair % 2 == 0:
+            for copy in returned(pair // 2):
+                copy.wait_recv()
+        columns = slice(pair * LANES, (pair + 1) * LANES)
+        near = own_mean[pair]
+        far_part = 1.0 / (1.0 + jnp.exp(own_lse[pair] - far_lse[pair]))
+        merged = near + (far_mean[pair].astype(jnp.float32) - near) * far_part
+        total = resid_ref[:, columns].astype(jnp.float32) + merged.astype(jnp.bfloat16).astype(
+            jnp.float32
+        )
+        residual[:, columns] = total
+        squares = squares + total * total
+    mean_square = jnp.sum(squares, axis=1, keepdims=True) / model
+    x[0, :rows, :model] = (
+        residual[...] * lax.rsqrt(mean_square + 1e-06) * gain_ref[...]
+    ).astype(jnp.bfloat16)
 
     def gather(hop, part):
         if isinstance(hop, int) and hop == hops:
@@ -346,11 +416,12 @@
             copy.wait_recv()
         some, rest = pl.ds(0, rows), pl.ds(rows, rows)
         out_ref[:, columns] = (
-            wider(o, 0, some, columns)
+            residual[:, columns]
+            + wider(o, 0, some, columns)
             + wider(sibling_sums, 0, some, columns)
             + wider(ring_sums, 0, some, columns)
             + wider(ring_sums, 0, rest, columns)
-        )
+        ).astype(out_ref.dtype)
 
     def sent(hop, count):
         for part in range(2):
@@ -359,6 +430,14 @@
             share(hop, count, part).wait_send()
             pair(hop, count, part).wait_send()
 
+    visit.wait_send()
+
+    def drained(j, unused):
+        for copy in returned(j):
+            copy.wait_send()
+        return unused
+
+    lax.fori_loop(0, pairs // 2, drained, 0)
     for part in range(2):
         share(0, rows, part).wait_send()
         pair(0, rows, part).wait_send()
@@ -388,22 +467,46 @@
 
 
 def fits(buffers):
-    return sum(2 * math.prod(shape) for shape, unused in buffers) < 44 * 1024 * 1024
-
-
-def routed_experts(first, w_gate, w_up, w_down, devices):
-    rows, wide = first.shape
+    return sum(2 * math.prod(shape) for shape, unused in buffers) < 32 * 1024 * 1024
+
+
+def whole_layer(
+    start, length, queries, cache, row_key_value, marked, resid, gain, shares,
+    w_gate, w_up, w_down, devices,
+):
+    rows = queries.shape[0]
     model, ff = w_gate.shape[1:]
+    wide = model + shares.shape[1]
     hops = devices // 4
+    pairs = queries.shape[1] // LANES
+    keys = -(-(cache.shape[0] + rows) // LANES) * LANES
     anywhere = pl.BlockSpec(memory_space=pl.ANY)
     vmem = pl.BlockSpec(memory_space=pltpu.VMEM)
+    smem = pl.BlockSpec(memory_space=pltpu.SMEM)
     dma = pltpu.SemaphoreType.DMA
+    half_doc = (pairs, rows, LANES)
     return pl.pallas_call(
         functools.partial(experts_kernel, devices),
-        out_shape=jax.ShapeDtypeStruct((rows, model), jnp.float32),
-        in_specs=[vmem, anywhere, anywhere, anywhere],
+        out_shape=jax.ShapeDtypeStruct((rows, model), jnp.bfloat16),
+        in_specs=[smem, smem] + [vmem] * 7 + [anywhere] * 3,
         out_specs=vmem,
         scratch_shapes=[
+            pltpu.VMEM((pairs, 4 * rows, LANES), jnp.bfloat16),
+            pltpu.VMEM((KEY_VALUE_HEADS, LANES, keys), jnp.bfloat16),
+            pltpu.VMEM((KEY_VALUE_HEADS, keys, LANES), jnp.bfloat16),
+            pltpu.VMEM((2, 4 * rows, keys), jnp.float32),
+            pltpu.VMEM((rows, queries.shape[1]), jnp.bfloat16),
+            pltpu.VMEM(half_doc, jnp.float32),
+            pltpu.VMEM(half_doc, jnp.float32),
+            pltpu.VMEM(half_doc, jnp.bfloat16),
+            pltpu.VMEM(half_doc, jnp.float32),
+            pltpu.VMEM(half_doc, jnp.bfloat16),
+            pltpu.VMEM(half_doc, jnp.float32),
+            pltpu.VMEM((rows, model), jnp.float32),
+            dma((2,)),
+        ]
+        + [dma((pairs // 2,))] * 4
+        + [
             pltpu.VMEM(shape, kind)
             for shape, kind in scratch_of(rows, wide, model, ff, devices)
         ]
@@ -411,15 +514,18 @@
         + [dma((2, 2, hops + 1)), dma((2, 2, hops + 1)), dma((2, hops + 1)), dma((2, hops + 1))]
         + [dma((2, hops + 1)), dma((2, hops + 1)), dma((2, 2, hops + 1)), dma((2, 2, hops + 1))],
         compiler_params=pltpu.CompilerParams(
-            collective_id=0, has_side_effects=True, vmem_limit_bytes=56 * 1024 * 1024
+            collective_id=0, has_side_effects=True, vmem_limit_bytes=58 * 1024 * 1024
         ),
         cost_estimate=pl.CostEstimate(
-            flops=6 * rows * devices * model * ff,
-            bytes_accessed=6 * model * ff,
+            flops=6 * rows * devices * model * ff + 8 * rows * model * keys,
+            bytes_accessed=6 * model * ff + 2 * cache.size,
             transcendentals=rows * devices * ff,
         ),
-        name="experts",
-    )(first, w_gate, w_up, w_down)
+        name="whole_layer",
+    )(
+        start, length, queries, cache, row_key_value, marked, resid, gain, shares,
+        w_gate, w_up, w_down,
+    )
 
 
 def local(
@@ -454,8 +560,15 @@
 
     length = lax.dynamic_slice_in_dim(lengths, doc_index, 1, 0)
     marked = lax.dynamic_index_in_dim(positions, doc_index, 0, keepdims=False)[:, None]
+    start = jnp.reshape(half_index * span, (1,)).astype(jnp.int32)
+    model, ff = w_gate.shape[1:]
+    if experts % 4 == 0 and fits(scratch_of(rows, model + shares.shape[1], model, ff, experts)):
+        return whole_layer(
+            start, length, query_rows, key_value_cache, row_key_value, marked, resid,
+            norm_gain[None, :], shares, w_gate, w_up, w_down, experts,
+        )
+
     visitor = swapped(query_rows, "wide", 0)
-    start = jnp.reshape(half_index * span, (1,)).astype(jnp.int32)
     means, lse = attention(
         jnp.concatenate([query_rows, visitor], axis=0),
         key_value_cache, row_key_value, start, length, marked,
@@ -476,10 +589,6 @@
     ).astype(jnp.bfloat16)
 
     first = jnp.concatenate([normed, shares], axis=1)
-    model, ff = w_gate.shape[1:]
-    if experts % 4 == 0 and fits(scratch_of(rows, first.shape[1], model, ff, experts)):
-        routed = routed_experts(first, w_gate, w_up, w_down, experts)
-        return (residual + routed).astype(jnp.bfloat16)
 
     gathered = lax.all_gather(first, "wide", axis=0, tiled=True)
     everyone = gathered[:, :model]

time: 85.3 us -> 83.1 us (0.974)
  Pallas kernels: 73 us -> 76 us
  other arithmetic: 4.37 us -> 2.8 us
  waiting for transfers between devices: 1.45 us -> 0 us
  starting transfers between devices: 1.09 us -> 0 us
  local copies, waits for them, and re-layouts: 4.91 us -> 3.9 us
    pallas_call x2 -> x1, Pallas kernels: 73 us -> 76 us  [whole_layer(): pl.pallas_call(functools.partial(experts_kernel, devices), out_shape=jax....]
    convert_element_type x2 -> x0, other arithmetic: 2.26 us -> none  [the longest x1 2 us: local(): return (residual + routed).astype(jnp.bfloat16)]
    ppermute x3 -> x0, waiting for transfers between devices: 1.45 us -> none  [swapped(): lax.ppermute(shard, axis, [(i, i ^ 1 << bit) for i in range(lax.axis_size...]
    ppermute x3 -> x0, starting transfers between devices: 1.09 us -> none  [swapped(): lax.ppermute(shard, axis, [(i, i ^ 1 << bit) for i in range(lax.axis_size...]
    unnamed x14 -> x3, local copies, waits for them, and re-layouts: 2.45 us -> 1.67 us
  transfers between devices with their start and end apart: 3 -> 0, of which waited for: 1 -> 0; matrix products, arithmetic and copies ran while one was open for 3% -> 0% of each run, Pallas kernels for 0% -> 0%
where the time goes in v4:
time: 83.1 us; the launch traced here: 82.8 us
  Pallas kernels  76 us (91%)
  local copies, waits for them, and re-layouts  3.9 us (5%)
  other arithmetic  2.8 us (3%)
    pallas_call x1, Pallas kernels, whole_layer(): pl.pallas_call(functools.partial(experts_kernel, devices), out_shape=jax....  76 us
    unnamed x3, local copies, waits for them, and re-layouts  1.67 us

profile of v4, /device:TPU:0, one launch (start us, length us, event | category | flops | bytes accessed | tf_op | source)
XLA Modules:
  0.0 82.8 jit_solution(8495450986663058336)
XLA Ops:
  0.0 0.0 copy-start
  0.0 1.2 %dynamic_slice.7.length_ref = s32[1]{0:T(128)} dynamic-slice(s32[8]{0:T(128)} %param.17, s32[]{:T(128)S(6)} %select_n.22), dynamic_slice_sizes={1} | dynamic-slice | bytes 12 | tf_op jit(solution)/shard_map/dynamic_slice | solution.py:561
  1.2 0.0 copy-done
  1.2 0.7 reduce_sum.18
  1.9 0.1 pad.2.clone
  2.0 0.7 broadcast_divide_fusion
  2.7 0.7 select_reduce_fusion
  3.4 0.1 copy.21
  3.5 0.1 copy.20
  3.6 0.7 maximum_maximum_fusion.shares_ref
  4.3 0.7 copy.22.marked_ref
  5.1 76.0 %whole_layer.1 = bf16[64,2048]{1,0:T(8,128)(2,1)} custom-call(s32[1]{0:T(128)} %bitcast.start_ref, s32[1]{0:T(128)} %dynamic_slice.7.length_ref, bf16[64,2048]{1,0:T(8,128)(2,1)} %q_ref.1, bf16[2048,512]{1,0:T(8,128)(2,1)} %cache_ref.1, bf16[64,512]{1,0:T(8,128)(2,1)} %rows_ref.1, s32[128,1]{1,0:T(8,128)} %copy.22.marked_ref, bf16[64,2048]{1,0:T(8,128)(2,1)} %resid_ref.1, ...), custom_call_target="tpu_custom_call" | custom-call | flops 11945377792 | bytes 11534336 | tf_op jit(solution)/shard_map/whole_layer/pallas_call | solution.py:488
  81.1 1.7 %copy.24 = bf16[64,2048]{1,0:T(8,128)(2,1)} copy(bf16[64,2048]{1,0:T(8,128)(2,1)} %whole_layer.1) | data formatting | bytes 524288
  (4 shorter events, 0.0 us)
Async XLA Ops:
  0.0 1.2 %copy-start = (s32[8,128]{1,0:T(8,128)S(1)}, s32[8,128]{1,0:T(8,128)}, u32[]{:S(2)}) copy-start(s32[8,128]{1,0:T(8,128)} %param.18) | copy-start | bytes 12292

commit v5 on v4

--- a/solution.py
+++ b/solution.py
@@ -32,18 +32,18 @@
     ).astype(jnp.bfloat16)
 
 
-def place_keys(start_ref, length_ref, cache_ref, rows_ref, marked_ref, k_scr, v_scr):
+def place_keys(start, length, cache_ref, rows_ref, marked, k_scr, v_scr):
     span = cache_ref.shape[0]
     own = rows_ref.shape[0]
     keys = k_scr.shape[2]
     width = KEY_VALUE_HEADS * HEAD_SIZE
 
     location = lane_index((1, keys))
-    place = start_ref[0] + location
+    place = start + location
     hit = jnp.max(
-        jnp.where(marked_ref[...] == place, 1.0, 0.0), axis=0, keepdims=True
+        jnp.where(marked == place.astype(jnp.float32), 1.0, 0.0), axis=0, keepdims=True
     )
-    in_cache = (place < length_ref[0]) & (hit == 0.0) & (location < span)
+    in_cache = (place < length) & (hit == 0.0) & (location < span)
     usable = in_cache | ((location >= span) & (location < span + own))
     bias = jnp.where(usable, 0.0, NEVER)
     row = lax.broadcasted_iota(jnp.int32, (HEAD_SIZE, keys), 0)
@@ -68,27 +68,29 @@
 
 def place_queries(q_ref, q_scr, first):
     rows = q_ref.shape[0]
-    stride = q_scr.shape[1] // 2
-    for pair in range(q_scr.shape[0]):
+    pairs = q_ref.shape[1] // LANES
+    joined = pairs // q_scr.shape[0]
+    stride = q_scr.shape[1] // (2 * joined)
+    for pair in range(pairs):
         slab = q_ref[:, pair * LANES : (pair + 1) * LANES].astype(jnp.float32) * (
             1.0 / math.sqrt(HEAD_SIZE)
         )
         for odd in range(2):
-            at = odd * stride + first
-            q_scr[pair, at : at + rows, :] = half_with_one(slab, odd)
-
-
-def attend(q_scr, k_scr, v_scr, s_scr, store, after_step):
-    pairs = q_scr.shape[0]
-    rows = q_scr.shape[1] // 2
-    group = pairs // KEY_VALUE_HEADS
-
-    def scores(pair, slot):
-        head = lax.div(pair, group)
-        s_scr[slot] = jnp.dot(q_scr[pair], k_scr[head], preferred_element_type=jnp.float32)
-
-    def finish(pair, slot):
-        head = lax.div(pair, group)
+            at = (2 * (pair % joined) + odd) * stride + first
+            q_scr[pair // joined, at : at + rows, :] = half_with_one(slab, odd)
+
+
+def attend(q_scr, k_scr, v_scr, s_scr, joined, store, after_step):
+    steps = q_scr.shape[0]
+    rows = q_scr.shape[1] // (2 * joined)
+    group = steps // KEY_VALUE_HEADS
+
+    def scores(step, slot):
+        head = lax.div(step, group)
+        s_scr[slot] = jnp.dot(q_scr[step], k_scr[head], preferred_element_type=jnp.float32)
+
+    def finish(step, slot):
+        head = lax.div(step, group)
         s = s_scr[slot]
         largest = jnp.max(s, axis=1, keepdims=True)
         p = jnp.exp(s - largest).astype(jnp.bfloat16)
@@ -97,37 +99,43 @@
         mean = summed / total
         lse = jnp.broadcast_to(largest + jnp.log(total), mean.shape)
         low = lane_index((rows, LANES)) < HEAD_SIZE
-        store(
-            pair,
-            jnp.where(low, mean[:rows], pltpu.roll(mean[rows:], HEAD_SIZE, 1)),
-            jnp.where(low, lse[:rows], lse[rows:]),
-        )
+        for i in range(joined):
+            even = slice(2 * i * rows, (2 * i + 1) * rows)
+            odd = slice((2 * i + 1) * rows, (2 * i + 2) * rows)
+            store(
+                step * joined + i,
+                jnp.where(low, mean[even], pltpu.roll(mean[odd], HEAD_SIZE, 1)),
+                jnp.where(low, lse[even], lse[odd]),
+            )
 
     scores(0, 0)
 
-    def step(j, unused):
+    def two_steps(j, unused):
         scores(2 * j + 1, 1)
         finish(2 * j, 0)
-        scores(jnp.minimum(2 * j + 2, pairs - 1), 0)
+        scores(jnp.minimum(2 * j + 2, steps - 1), 0)
         finish(2 * j + 1, 1)
         after_step(j)
         return unused
 
-    lax.fori_loop(0, pairs // 2, step, 0)
+    lax.fori_loop(0, steps // 2, two_steps, 0)
 
 
 def attention_kernel(
     start_ref, length_ref, q_ref, cache_ref, rows_ref, marked_ref, out_ref, lse_ref,
     q_scr, k_scr, v_scr, s_scr,
 ):
-    place_keys(start_ref, length_ref, cache_ref, rows_ref, marked_ref, k_scr, v_scr)
+    place_keys(
+        start_ref[0], length_ref[0], cache_ref, rows_ref,
+        marked_ref[...].astype(jnp.float32), k_scr, v_scr,
+    )
     place_queries(q_ref, q_scr, 0)
 
     def store(pair, mean, lse):
         out_ref[pair] = mean.astype(jnp.bfloat16)
         lse_ref[pair] = lse
 
-    attend(q_scr, k_scr, v_scr, s_scr, store, lambda j: None)
+    attend(q_scr, k_scr, v_scr, s_scr, 1, store, lambda j: None)
 
 
 def attention(queries, cache, row_key_value, start, length, marked):
@@ -169,8 +177,8 @@
 
 
 def experts_kernel(
-    devices, start_ref, length_ref, q_ref, cache_ref, rows_ref, marked_ref,
-    resid_ref, gain_ref, shares_ref, gate_hbm, up_hbm, down_hbm, out_ref,
+    devices, joined, lengths_ref, q_ref, cache_ref, rows_ref, positions_ref,
+    resid_ref, gain_ref, ids_ref, gates_ref, gate_hbm, up_hbm, down_hbm, out_ref,
     q_scr, k_scr, v_scr, s_scr, visitor, own_mean, own_lse, host_mean, host_lse,
     far_mean, far_lse, residual,
     visit_sem, mean_send, mean_recv, lse_send, lse_recv,
@@ -207,7 +215,17 @@
     ]
     for load in loads:
         load.start()
-    x[0, :rows, model:] = shares_ref[...]
+    gates = gates_ref[...]
+    mix = gates / jnp.sum(gates, axis=1, keepdims=True)
+    lane = lane_index((rows, x.shape[2] - model))
+    high = jnp.zeros(lane.shape, jnp.float32)
+    low = jnp.zeros(lane.shape, jnp.float32)
+    for choice in range(ids_ref.shape[1]):
+        expert, amount = ids_ref[:, choice : choice + 1], mix[:, choice : choice + 1]
+        high = high + jnp.where(lane == expert, amount, 0.0)
+        low = low + jnp.where(lane == expert + devices, amount, 0.0)
+    low = low - low.astype(jnp.bfloat16).astype(jnp.float32)
+    x[0, :rows, model:] = (high + low).astype(jnp.bfloat16)
     ring_sums[hops - 1, half : rows + half] = jnp.zeros((rows, model), jnp.bfloat16)
 
     barrier = pltpu.get_barrier_semaphore()
@@ -219,7 +237,13 @@
 
     visit = remote(q_ref, visitor, visit_sem.at[0], visit_sem.at[1], sibling)
     visit.start()
-    place_keys(start_ref, length_ref, cache_ref, rows_ref, marked_ref, k_scr, v_scr)
+    document = me // 2
+    marked = positions_ref[pl.ds(document, 1), :].astype(jnp.float32)
+    marked = jnp.broadcast_to(marked, (LANES, marked.shape[1])).T[:, :1]
+    place_keys(
+        core * cache_ref.shape[0], lengths_ref[document], cache_ref, rows_ref, marked,
+        k_scr, v_scr,
+    )
     place_queries(q_ref, q_scr, 0)
     visit.wait_recv()
     place_queries(visitor, q_scr, rows)
@@ -231,7 +255,7 @@
         host_lse[pair] = lse[rows:]
 
     def returned(j):
-        two = pl.ds(2 * j, 2)
+        two = pl.ds(2 * joined * j, 2 * joined)
         return (
             remote(host_mean.at[two], far_mean.at[two], mean_send.at[j], mean_recv.at[j], sibling),
             remote(host_lse.at[two], far_lse.at[two], lse_send.at[j], lse_recv.at[j], sibling),
@@ -241,13 +265,13 @@
         for copy in returned(j):
             copy.start()
 
-    attend(q_scr, k_scr, v_scr, s_scr, store, send_back)
-
-    pairs = q_scr.shape[0]
+    attend(q_scr, k_scr, v_scr, s_scr, joined, store, send_back)
+
+    pairs = own_mean.shape[0]
     squares = jnp.zeros((rows, LANES), jnp.float32)
     for pair in range(pairs):
-        if pair % 2 == 0:
-            for copy in returned(pair // 2):
+        if pair % (2 * joined) == 0:
+            for copy in returned(pair // (2 * joined)):
                 copy.wait_recv()
         columns = slice(pair * LANES, (pair + 1) * LANES)
         near = own_mean[pair]
@@ -437,7 +461,7 @@
             copy.wait_send()
         return unused
 
-    lax.fori_loop(0, pairs // 2, drained, 0)
+    lax.fori_loop(0, pairs // (2 * joined), drained, 0)
     for part in range(2):
         share(0, rows, part).wait_send()
         pair(0, rows, part).wait_send()
@@ -470,13 +494,17 @@
     return sum(2 * math.prod(shape) for shape, unused in buffers) < 32 * 1024 * 1024
 
 
+def share_width(devices):
+    return -(-2 * devices // LANES) * LANES
+
+
 def whole_layer(
-    start, length, queries, cache, row_key_value, marked, resid, gain, shares,
+    lengths, queries, cache, row_key_value, positions, resid, gain, ids, gates,
     w_gate, w_up, w_down, devices,
 ):
     rows = queries.shape[0]
     model, ff = w_gate.shape[1:]
-    wide = model + shares.shape[1]
+    wide = model + share_width(devices)
     hops = devices // 4
     pairs = queries.shape[1] // LANES
     keys = -(-(cache.shape[0] + rows) // LANES) * LANES
@@ -485,16 +513,17 @@
     smem = pl.BlockSpec(memory_space=pltpu.SMEM)
     dma = pltpu.SemaphoreType.DMA
     half_doc = (pairs, rows, LANES)
+    joined = 2 if pairs % (4 * KEY_VALUE_HEADS) == 0 else 1
     return pl.pallas_call(
-        functools.partial(experts_kernel, devices),
+        functools.partial(experts_kernel, devices, joined),
         out_shape=jax.ShapeDtypeStruct((rows, model), jnp.bfloat16),
-        in_specs=[smem, smem] + [vmem] * 7 + [anywhere] * 3,
+        in_specs=[smem] + [vmem] * 8 + [anywhere] * 3,
         out_specs=vmem,
         scratch_shapes=[
-            pltpu.VMEM((pairs, 4 * rows, LANES), jnp.bfloat16),
+            pltpu.VMEM((pairs // joined, 4 * joined * rows, LANES), jnp.bfloat16),
             pltpu.VMEM((KEY_VALUE_HEADS, LANES, keys), jnp.bfloat16),
             pltpu.VMEM((KEY_VALUE_HEADS, keys, LANES), jnp.bfloat16),
-            pltpu.VMEM((2, 4 * rows, keys), jnp.float32),
+            pltpu.VMEM((2, 4 * joined * rows, keys), jnp.float32),
             pltpu.VMEM((rows, queries.shape[1]), jnp.bfloat16),
             pltpu.VMEM(half_doc, jnp.float32),
             pltpu.VMEM(half_doc, jnp.float32),
@@ -505,7 +534,7 @@
             pltpu.VMEM((rows, model), jnp.float32),
             dma((2,)),
         ]
-        + [dma((pairs // 2,))] * 4
+        + [dma((pairs // (2 * joined),))] * 4
         + [
             pltpu.VMEM(shape, kind)
             for shape, kind in scratch_of(rows, wide, model, ff, devices)
@@ -523,7 +552,7 @@
         ),
         name="whole_layer",
     )(
-        start, length, queries, cache, row_key_value, marked, resid, gain, shares,
+        lengths, queries, cache, row_key_value, positions, resid, gain, ids, gates,
         w_gate, w_up, w_down,
     )
 
@@ -550,6 +579,14 @@
     doc_index = device // 2
     half_index = device % 2
 
+    model, ff = w_gate.shape[1:]
+    buffers = scratch_of(rows, model + share_width(experts), model, ff, experts)
+    if experts % 4 == 0 and fits(buffers):
+        return whole_layer(
+            lengths, query_rows, key_value_cache, row_key_value, positions, resid,
+            norm_gain[None, :], expert_ids, gate_scores, w_gate, w_up, w_down, experts,
+        )
+
     mix = gate_scores / jnp.sum(gate_scores, axis=-1, keepdims=True)
     chosen = expert_ids[..., None] == jnp.arange(experts, dtype=jnp.int32)
     share = jnp.sum(jnp.where(chosen, mix[..., None], 0.0), axis=1)
@@ -561,13 +598,6 @@
     length = lax.dynamic_slice_in_dim(lengths, doc_index, 1, 0)
     marked = lax.dynamic_index_in_dim(positions, doc_index, 0, keepdims=False)[:, None]
     start = jnp.reshape(half_index * span, (1,)).astype(jnp.int32)
-    model, ff = w_gate.shape[1:]
-    if experts % 4 == 0 and fits(scratch_of(rows, model + shares.shape[1], model, ff, experts)):
-        return whole_layer(
-            start, length, query_rows, key_value_cache, row_key_value, marked, resid,
-            norm_gain[None, :], shares, w_gate, w_up, w_down, experts,
-        )
-
     visitor = swapped(query_rows, "wide", 0)
     means, lse = attention(
         jnp.concatenate([query_rows, visitor], axis=0),

time: 83.1 us -> 78.8 us (0.948)
  other arithmetic: 2.8 us -> 0 us
  Pallas kernels: 76 us -> 74.1 us
    unnamed x3, local copies, waits for them, and re-layouts: 1.67 us -> 4.42 us
    pallas_call x1, Pallas kernels: 76 us -> 74.1 us  [whole_layer(): pl.pallas_call(functools.partial(experts_kernel, devices, joined), out_sh...]
    reduce_sum x2 -> x0, other arithmetic: 1.41 us -> none  [the longest x1 0.71 us: local(): share = jnp.sum(jnp.where(chosen, mix[..., None], 0.0), axis=1)]
    dynamic_slice x1 -> x0, local copies, waits for them, and re-layouts: 1.22 us -> none  [local(): length = lax.dynamic_slice_in_dim(lengths, doc_index, 1, 0)]
where the time goes in v5:
time: 78.8 us; the launch traced here: 78.6 us
  Pallas kernels  74.1 us (94%)
  local copies, waits for them, and re-layouts  4.42 us (6%)
    pallas_call x1, Pallas kernels, whole_layer(): pl.pallas_call(functools.partial(experts_kernel, devices, joined), out_sh...  74.1 us
    unnamed x3, local copies, waits for them, and re-layouts  4.42 us

profile of v5, /device:TPU:0, one launch (start us, length us, event | category | flops | bytes accessed | tf_op | source)
XLA Modules:
  0.0 78.6 jit_solution(14941050152258561051)
XLA Ops:
  0.0 1.4 %copy.13.ids_ref = s32[64,8]{1,0:T(8,128)} copy(s32[64,8]{0,1:T(8,128)} %param.19) | data formatting | bytes 4096 | tf_op args[7]
  1.4 1.4 %copy.14.gates_ref = f32[64,8]{1,0:T(8,128)} copy(f32[64,8]{0,1:T(8,128)} %param.20) | data formatting | bytes 4096 | tf_op args[8]
  2.8 74.1 %whole_layer.1 = bf16[64,2048]{1,0:T(8,128)(2,1)} custom-call(s32[8]{0:T(128)} %lengths_ref.1, bf16[64,2048]{1,0:T(8,128)(2,1)} %q_ref.1, bf16[2048,512]{1,0:T(8,128)(2,1)} %cache_ref.1, bf16[64,512]{1,0:T(8,128)(2,1)} %rows_ref.1, s32[8,128]{1,0:T(8,128)} %positions_ref.1, bf16[64,2048]{1,0:T(8,128)(2,1)} %resid_ref.1, f32[1,2048]{1,0:T(1,128)} %bitcast.1, ...), custom_call_target="tpu_custom_call" | custom-call | flops 11945377792 | bytes 11534336 | tf_op jit(solution)/shard_map/whole_layer/pallas_call | solution.py:517
  76.9 1.7 %copy.16 = bf16[64,2048]{1,0:T(8,128)(2,1)} copy(bf16[64,2048]{1,0:T(8,128)(2,1)} %whole_layer.1) | data formatting | bytes 524288

commit v6 on v5

--- a/solution.py
+++ b/solution.py
@@ -215,13 +215,14 @@
     ]
     for load in loads:
         load.start()
-    gates = gates_ref[...]
+    gates = gates_ref[...].T
+    ids = ids_ref[...].astype(jnp.float32).T
     mix = gates / jnp.sum(gates, axis=1, keepdims=True)
-    lane = lane_index((rows, x.shape[2] - model))
+    lane = lane_index((rows, x.shape[2] - model)).astype(jnp.float32)
     high = jnp.zeros(lane.shape, jnp.float32)
     low = jnp.zeros(lane.shape, jnp.float32)
-    for choice in range(ids_ref.shape[1]):
-        expert, amount = ids_ref[:, choice : choice + 1], mix[:, choice : choice + 1]
+    for choice in range(ids.shape[1]):
+        expert, amount = ids[:, choice : choice + 1], mix[:, choice : choice + 1]
         high = high + jnp.where(lane == expert, amount, 0.0)
         low = low + jnp.where(lane == expert + devices, amount, 0.0)
     low = low - low.astype(jnp.bfloat16).astype(jnp.float32)
@@ -584,7 +585,7 @@
     if experts % 4 == 0 and fits(buffers):
         return whole_layer(
             lengths, query_rows, key_value_cache, row_key_value, positions, resid,
-            norm_gain[None, :], expert_ids, gate_scores, w_gate, w_up, w_down, experts,
+            norm_gain[None, :], expert_ids.T, gate_scores.T, w_gate, w_up, w_down, experts,
         )
 
     mix = gate_scores / jnp.sum(gate_scores, axis=-1, keepdims=True)

time: 78.8 us -> 76.4 us (0.970)
  local copies, waits for them, and re-layouts: 4.42 us -> 1.67 us
    unnamed x3 -> x1, local copies, waits for them, and re-layouts: 4.42 us -> 1.67 us
where the time goes in v6:
time: 76.4 us; the launch traced here: 76.2 us
  Pallas kernels  74.5 us (98%)
  local copies, waits for them, and re-layouts  1.67 us (2%)
    pallas_call x1, Pallas kernels, whole_layer(): pl.pallas_call(functools.partial(experts_kernel, devices, joined), out_sh...  74.5 us
    unnamed x1, local copies, waits for them, and re-layouts  1.67 us

profile of v6, /device:TPU:0, one launch (start us, length us, event | category | flops | bytes accessed | tf_op | source)
XLA Modules:
  0.0 76.2 jit_solution(2774808602537055376)
XLA Ops:
  0.0 74.5 %whole_layer.1 = bf16[64,2048]{1,0:T(8,128)(2,1)} custom-call(s32[8]{0:T(128)} %lengths_ref.1, bf16[64,2048]{1,0:T(8,128)(2,1)} %q_ref.1, bf16[2048,512]{1,0:T(8,128)(2,1)} %cache_ref.1, bf16[64,512]{1,0:T(8,128)(2,1)} %rows_ref.1, s32[8,128]{1,0:T(8,128)} %positions_ref.1, bf16[64,2048]{1,0:T(8,128)(2,1)} %resid_ref.1, f32[1,2048]{1,0:T(1,128)} %bitcast.3, ...), custom_call_target="tpu_custom_call" | custom-call | flops 11945377792 | bytes 11534336 | tf_op jit(solution)/shard_map/whole_layer/pallas_call | solution.py:518
  74.5 1.7 %copy.14 = bf16[64,2048]{1,0:T(8,128)(2,1)} copy(bf16[64,2048]{1,0:T(8,128)(2,1)} %whole_layer.1) | data formatting | bytes 524288
